TPU v7x, 256 devices: a whole 4x4x8 slice. The times are simulated.
256 devices in a mesh: dom: 64 (over x_lo, z, y), edge: 4 (over x_hi, core).
Axes of the slice: x: 4 (x_hi: 2, x_lo: 2; x = x_hi * 2 + x_lo), y: 4, z: 8, core: 2. Of those that a mesh axis runs over, the one named last changes fastest.
Arguments:
- entity_emb: float32 [131072, 400], P('dom'), may hold values from -3 to 3
- entity_state: float32 [131072], P('dom'), may hold values from 4 to 1000
- relation_emb: float32 [7424, 400], P(('dom', 'edge')), may hold values from -1.5 to 1.5
- relation_state: float32 [7424], P(('dom', 'edge')), may hold values from 4 to 1000
- head_rows: int32 [2, 131072], P(None, ('dom', 'edge')), may hold values from 0 to 2047
- tail_rows: int32 [2, 131072], P(None, ('dom', 'edge')), may hold values from 0 to 2047
- relation_ids: int32 [2, 131072], P(None, ('dom', 'edge')), may hold values from 0 to 7423
- negative_rows: int32 [2, 256, 256], P(None, ('dom', 'edge')), may hold values from 0 to 2047
Outputs:
- new_entity_emb: float32 [131072, 400], P('dom')
- new_entity_state: float32 [131072], P('dom')
- new_relation_emb: float32 [7424, 400], P(('dom', 'edge'))
- new_relation_state: float32 [7424], P(('dom', 'edge'))
All inputs are finite; a program needn't handle non-finite values.
Results may differ from a plain program's by a relative error of at most 0.0063.
Values may be sent and summed in bfloat16 or wider, within the bound.
A program may use at most 128 MiB of HBM per device.

v0:
```python
import jax
import jax.numpy as jnp
from jax import lax
from jax.sharding import PartitionSpec as P

LEARN_RATE = 0.5


def shifted(value, axis, steps):
    count = lax.axis_size(axis)
    pairs = [(source, (source + steps) % count) for source in range(count)]
    return lax.ppermute(value, axis, pairs)


def complex_times(left_side, right_side):
    middle = left_side.shape[-1] // 2
    left_real, left_imag = (left_side[..., :middle], left_side[..., middle:])
    right_real, right_imag = (right_side[..., :middle], right_side[..., middle:])
    return jnp.concatenate(
        [
            left_real * right_real - left_imag * right_imag,
            left_real * right_imag + left_imag * right_real,
        ],
        axis=-1,
    )


def complex_back(upstream, head_vec, rel_vec):
    middle = upstream.shape[-1] // 2
    up_real, up_imag = (upstream[..., :middle], upstream[..., middle:])
    head_real, head_imag = (head_vec[..., :middle], head_vec[..., middle:])
    rel_real, rel_imag = (rel_vec[..., :middle], rel_vec[..., middle:])
    head_grad = jnp.concatenate(
        [up_real * rel_real + up_imag * rel_imag, up_imag * rel_real - up_real * rel_imag], axis=-1
    )
    rel_grad = jnp.concatenate(
        [up_real * head_real + up_imag * head_imag, up_imag * head_real - up_real * head_imag],
        axis=-1,
    )
    return (head_grad, rel_grad)


def bucket_terms(
    own_rows, partner_rows, relation_table, head_ids, tail_ids, relation_index, negatives
):
    part_rows, features = own_rows.shape
    head_vec = own_rows[head_ids].astype(jnp.float32)
    tail_low = partner_rows[tail_ids]
    rel_vec = relation_table[relation_index].astype(jnp.float32)
    queries = complex_times(head_vec, rel_vec)
    queries_low = queries.astype(jnp.bfloat16)
    positive = jnp.sum(queries * tail_low.astype(jnp.float32), axis=-1)
    blocks = negatives.shape[0]
    sampled_entities = partner_rows[negatives]
    grouped_rows = queries_low.reshape(blocks, -1, features)
    triple_scores = jnp.einsum(
        "ymt,yst->yms", grouped_rows, sampled_entities, preferred_element_type=jnp.float32
    )
    pos_slope = -jax.nn.sigmoid(-positive)
    negative_gradient = jax.nn.sigmoid(triple_scores).astype(jnp.bfloat16)
    gathered_rows = jnp.einsum(
        "zsm,zmi->zsi", negative_gradient, sampled_entities, preferred_element_type=jnp.float32
    )
    query_grad = pos_slope[:, None] * tail_low.astype(jnp.float32) + gathered_rows.reshape(
        -1, features
    )
    negative_sample_gradient = jnp.einsum(
        "tyo,tyv->tov", negative_gradient, grouped_rows, preferred_element_type=jnp.float32
    )
    head_grad, rel_grad = complex_back(query_grad, head_vec, rel_vec)
    own_grad = jnp.zeros((part_rows, features), jnp.float32).at[head_ids].add(head_grad)
    partner_grad = (
        jnp.zeros((part_rows, features), jnp.float32).at[tail_ids].add(pos_slope[:, None] * queries)
    )
    partner_grad = partner_grad.at[negatives.reshape(-1)].add(
        negative_sample_gradient.reshape(-1, features)
    )
    return (own_grad, partner_grad, rel_grad)


def adagrad(weights, history, gradient):
    new_history = history + jnp.mean(gradient * gradient, axis=-1)
    return (weights - LEARN_RATE * gradient / jnp.sqrt(new_history)[:, None], new_history)


def local(
    entity_emb,
    entity_state,
    relation_emb,
    relation_state,
    head_rows,
    tail_rows,
    relation_ids,
    negative_rows,
):
    part_rows, features = entity_emb.shape
    own_low = entity_emb.astype(jnp.bfloat16)
    relation_table = lax.all_gather(
        relation_emb.astype(jnp.bfloat16), ("dom", "edge"), axis=0, tiled=True
    )
    upper_rows = shifted(own_low, "dom", -1)
    lower_rows = shifted(own_low, "dom", 1)
    own_first, upper_grad, rel_first = bucket_terms(
        own_low,
        upper_rows,
        relation_table,
        head_rows[0],
        tail_rows[0],
        relation_ids[0],
        negative_rows[0],
    )
    own_second, lower_grad, rel_second = bucket_terms(
        own_low,
        lower_rows,
        relation_table,
        head_rows[1],
        tail_rows[1],
        relation_ids[1],
        negative_rows[1],
    )
    from_lower = shifted(upper_grad.astype(jnp.bfloat16), "dom", 1)
    from_upper = shifted(lower_grad.astype(jnp.bfloat16), "dom", -1)
    local_total = (
        own_first + own_second + from_lower.astype(jnp.float32) + from_upper.astype(jnp.float32)
    )
    entity_grad = lax.psum(local_total, "edge")
    new_entity_emb, new_entity_state = adagrad(entity_emb, entity_state, entity_grad)
    all_ids = jnp.concatenate([relation_ids[0], relation_ids[1]], axis=0)
    all_grads = jnp.concatenate([rel_first, rel_second], axis=0)
    rel_total = relation_table.shape[0]
    own_count = relation_emb.shape[0]
    edge_count = lax.axis_size("edge")
    dom_count = lax.axis_size("dom")
    grad_table = jnp.zeros((rel_total, features), jnp.float32).at[all_ids].add(all_grads)
    arranged = grad_table.reshape(dom_count, edge_count * own_count, features)
    received = lax.all_to_all(arranged, "dom", split_axis=0, concat_axis=0, tiled=True)
    group_total = jnp.sum(received, axis=0)
    relation_grad = lax.psum_scatter(group_total, "edge", scatter_dimension=0, tiled=True)
    new_relation_emb, new_relation_state = adagrad(relation_emb, relation_state, relation_grad)
    return (new_entity_emb, new_entity_state, new_relation_emb, new_relation_state)


def solution(mesh):
    placed = (
        P("dom", None),
        P("dom"),
        P(("dom", "edge"), None),
        P(("dom", "edge")),
        P(None, ("dom", "edge")),
        P(None, ("dom", "edge")),
        P(None, ("dom", "edge")),
        P(None, ("dom", "edge"), None),
    )
    return jax.shard_map(
        local,
        mesh=mesh,
        in_specs=placed,
        out_specs=(P("dom", None), P("dom"), P(("dom", "edge"), None), P(("dom", "edge"))),
        check_vma=False,
    )
```

profile of v0, /device:TPU:1, one launch (start us, length us, event | category | flops | bytes accessed | tf_op | source)
XLA Modules:
  0.0 1024.1 jit_solution(2868409708853733382)
XLA Ops:
  8.7 3.3 convert_element_type.58
  14.2 7.7 collective-permute-start
  21.8 2.8 copy.64
  30.3 27.4 %collective-permute-done.2 = bf16[2048,400]{0,1:T(8,128)(2,1)} collective-permute-done((bf16[2048,400]{0,1:T(8,128)(2,1)}, bf16[2048,400]{0,1:T(8,128)(2,1)}, u32[]{:S(2)}, u32[]{:S(2)}) %collective-permute-start.2) | collective-permute-done | bytes 1638432 | tf_op jit(solution)/shard_map/ppermute | solution.py:12
  57.7 2.8 copy.76
  66.2 2.8 copy.67
  75.4 384.2 %all-gather.3.cloned.1.call-done = bf16[256,29,400]{2,1,0:T(8,128)(2,1)} async-done(((bf16[1,29,400]{2,1,0:T(8,128)(2,1)}), bf16[256,29,400]{2,1,0:T(8,128)(2,1)}) %all-gather.3.cloned.1.call-update) | async-done | bytes 5939216 | tf_op jit(solution)/shard_map/all_gather | solution.py:98
  459.6 11.4 %reshape.596 = bf16[7424,400]{1,0:T(8,128)(2,1)} reshape(bf16[256,29,400]{2,1,0:T(8,128)(2,1)} %all-gather.3.cloned.1.call-done) | data formatting | bytes 11878400
  471.0 6.2 gather_fusion.5
  479.5 6.6 gather_fusion.1
  496.4 13.6 %scatter_custom_fusion.5 = f32[7424,400]{1,0:T(8,128)} fusion(s32[1024]{0:T(1024)S(1)} %bitcast.60, f32[1024,400]{1,0:T(8,128)} %copy.85, f32[]{:T(128)} %constant.7.clone.1), kind=kCustom, calls=%fused_computation.14 | custom fusion | flops 409600 | bytes 11878912 | tf_op jit(solution)/shard_map/scatter-add | solution.py:134
  510.0 15.1 %reshape.597 = f32[64,116,400]{2,1,0:T(8,128)} reshape(f32[7424,400]{1,0:T(8,128)} %scatter_custom_fusion.5) | data formatting | bytes 23756800 | tf_op jit(solution)/shard_map/reshape | solution.py:135
  525.1 16.2 %copy.87 = f32[64,116,400]{1,2,0:T(8,128)} copy(f32[64,116,400]{2,1,0:T(8,128)} %reshape.597) | data formatting | bytes 23756800 | tf_op jit(solution)/shard_map/reshape | solution.py:135
  541.3 7.1 all-to-all-start
  549.8 6.6 scatter_custom_fusion.2
  556.7 6.2 scatter_fusion.1
  562.9 4.4 copy.81
  567.3 5.5 collective-permute-start.3
  573.1 5.7 scatter_custom_fusion
  579.2 6.2 scatter_fusion
  585.4 3.3 copy.72
  592.3 270.7 %collective-permute-done.3 = bf16[2048,400]{0,1:T(8,128)(2,1)} collective-permute-done((bf16[2048,400]{0,1:T(8,128)(2,1)}, bf16[2048,400]{0,1:T(8,128)(2,1)}, u32[]{:S(2)}, u32[]{:S(2)}) %collective-permute-start.3) | collective-permute-done | bytes 1638432 | tf_op jit(solution)/shard_map/ppermute | solution.py:12
  863.0 5.9 collective-permute-done.1
  871.4 3.3 copy.82
  874.7 11.3 %scatter_fusion.2 = f32[2048,400]{1,0:T(8,128)} fusion(f32[2048,400]{1,0:T(8,128)} %copy.82, s32[1024]{0:T(1024)S(1)} %bitcast.51, f32[1024,400]{1,0:T(8,128)} %copy.83), kind=kCustom, calls=%fused_computation.12 | custom fusion | flops 409600 | bytes 4919296 | tf_op jit(solution)/shard_map/add | solution.py:124
  888.0 3.3 copy.84
  892.5 88.1 %all-reduce.4.cloned.1.call-done = f32[2048,400]{1,0:T(8,128)} async-done(((f32[2048,400]{1,0:T(8,128)}), f32[2048,400]{1,0:T(8,128)}) %all-reduce.4.cloned.1.call-update) | async-done | bytes 3276816 | tf_op jit(solution)/shard_map/psum | solution.py:126
  983.8 5.6 reduce_sum.48
  989.6 8.8 fusion
  998.4 5.8 collective-permute-start.4
  1004.2 6.1 divide_subtract_fusion
  1010.3 5.2 copy.90
  (128 shorter events, 49.7 us)
Async XLA Ops:
  7.2 452.4 %all-gather.3.cloned.1.call-start = ((), (), s32[]{:S(2)}) async-start(), calls=%async_computation.2 | async-start | bytes 8421376 | tf_op jit(solution)/shard_map/all_gather | solution.py:98
  8.7 15.9 %copy-start.24 = (s32[2,512]{1,0:T(2,128)S(1)}, s32[2,512]{1,0:T(2,128)}, u32[]{:S(2)}) copy-start(s32[2,512]{1,0:T(2,128)} %param.12) | copy-start | bytes 12292
  12.0 45.7 %collective-permute-start.2 = (bf16[2048,400]{0,1:T(8,128)(2,1)}, bf16[2048,400]{0,1:T(8,128)(2,1)}, u32[]{:S(2)}, u32[]{:S(2)}) collective-permute-start(bf16[2048,400]{0,1:T(8,128)(2,1)} %convert_element_type.58), channel_id=1, source_target_pairs={{0,4},{4,8},{8,12},{12,16},{16,20},{20,24},{24,28},{28,32},{32,36}... | collective-permute-start | bytes 4915208 | tf_op jit(solution)/shard_map/ppermute | solution.py:12
  14.2 52.0 %collective-permute-start = (bf16[2048,400]{0,1:T(8,128)(2,1)}, bf16[2048,400]{0,1:T(8,128)(2,1)}, u32[]{:S(2)}, u32[]{:S(2)}) collective-permute-start(bf16[2048,400]{0,1:T(8,128)(2,1)} %convert_element_type.58), channel_id=1, source_target_pairs={{0,252},{4,0},{8,4},{12,8},{16,12},{20,16},{24,20},{28,24},{32,28}... | collective-permute-start | bytes 4915208 | tf_op jit(solution)/shard_map/ppermute | solution.py:12
  27.9 2.3 copy-start.25
  27.9 2.3 copy-start.21
  27.9 2.4 copy-start.22
  64.3 413.3 %copy-start.9 = (bf16[512,400]{0,1:T(8,128)(2,1)}, bf16[512,400]{0,1:T(8,128)(2,1)S(1)}, u32[]{:S(2)}) copy-start(bf16[512,400]{0,1:T(8,128)(2,1)S(1)} %copy.77) | copy-start | bytes 1228804
  471.0 6.5 copy-start.1
  477.6 8.4 copy-start.2
  487.0 1.4 copy-start.8
  487.0 1.6 copy-start.17
  488.2 1.2 copy-start.10
  488.2 1.3 copy-start.15
  488.2 1.4 copy-start.19
  489.6 2.4 copy-start.13
  541.3 7.2 copy-start.12
  541.3 442.6 %all-to-all-start = ((f32[64,116,400]{1,2,0:T(8,128)}), f32[64,116,400]{1,2,0:T(8,128)}, u32[]{:S(2)}, u32[]{:S(2)}) async-start(f32[64,116,400]{1,2,0:T(8,128)} %copy.87), calls=%async_computation | async-start | bytes 26214400 | tf_op jit(solution)/shard_map/all_to_all | solution.py:136
  548.4 8.0 copy-start.4
  548.4 8.0 copy-start.7
  548.4 8.0 copy-start.16
  548.4 432.2 %all-reduce.4.cloned.1.call-start = ((), (), s32[]{:S(2)}) async-start(), calls=%async_computation.1 | async-start | bytes 8388608 | tf_op jit(solution)/shard_map/psum | solution.py:126
  562.9 9.9 copy-start.11
  567.3 11.6 %copy-start.14 = (bf16[512,256]{1,0:T(8,128)(2,1)S(1)}, bf16[512,256]{1,0:T(8,128)(2,1)}, u32[]{:S(2)}) copy-start(bf16[512,256]{1,0:T(8,128)(2,1)} %copy-done.13) | copy-start | bytes 786436
  567.3 295.7 %collective-permute-start.3 = (bf16[2048,400]{0,1:T(8,128)(2,1)}, bf16[2048,400]{0,1:T(8,128)(2,1)}, u32[]{:S(2)}, u32[]{:S(2)}) collective-permute-start(bf16[2048,400]{0,1:T(8,128)(2,1)} %copy.81), channel_id=1, source_target_pairs={{0,252},{4,0},{8,4},{12,8},{16,12},{20,16},{24,20},{28,24},{32,28}... | collective-permute-start | bytes 4915208 | tf_op jit(solution)/shard_map/ppermute | solution.py:12
  588.7 280.2 %collective-permute-start.1 = (bf16[2048,400]{0,1:T(8,128)(2,1)S(1)}, bf16[2048,400]{0,1:T(8,128)(2,1)}, u32[]{:S(2)}, u32[]{:S(2)}) collective-permute-start(bf16[2048,400]{0,1:T(8,128)(2,1)S(1)} %copy.72), channel_id=1, source_target_pairs={{0,4},{4,8},{8,12},{12,16},{16,20},{20,24},{24,28},{28,32},{32,36}... | collective-permute-start | bytes 4915208 | tf_op jit(solution)/shard_map/ppermute | solution.py:12
  886.1 1.9 copy-start
  888.0 3.3 copy-start.27
  891.3 91.9 %copy-start.23 = (f32[2048]{0:T(1024)S(1)}, f32[2048]{0:T(1024)}, u32[]{:S(2)}) copy-start(f32[2048]{0:T(1024)} %param.9) | copy-start | bytes 24580
  998.4 17.1 %collective-permute-start.4 = (f32[9,400]{1,0:T(8,128)S(1)}, f32[9,400]{1,0:T(8,128)S(1)}, u32[]{:S(2)}, u32[]{:S(2)}) collective-permute-start(f32[9,400]{1,0:T(8,128)S(1)} %slice.118), channel_id=1, source_target_pairs={{0,1},{1,2},{2,3},{4,5},{5,6},{6,7},{8,9},{9,10},{10,11},{12,13},{... | collective-permute-start | bytes 43208
  1010.3 5.5 copy-start.26
  1010.3 6.1 copy-start.20
  (4 other events, 4.0 us)
Sparse Core Ops, SparseCore 0:
  10.5 449.0 all-gather.2
  886.2 94.4 all-reduce.3
where the time goes:
time: 1040 us; the launch traced here: 1020 us
  waiting for transfers between devices  776 us (75%)
  local copies, waits for them, and re-layouts  110 us (11%)
  other arithmetic  80.3 us (8%)
  starting transfers between devices  28.5 us (3%)
  between operations  15.5 us (1%)
    all_gather x1, waiting for transfers between devices, local(): lax.all_gather(relation_emb.astype(jnp.bfloat16), ('dom', 'edge'), axis=0...  384 us
    ppermute x4, waiting for transfers between devices, shifted(): return lax.ppermute(value, axis, pairs)  304 us
    psum x1, waiting for transfers between devices, local(): entity_grad = lax.psum(local_total, 'edge')  88.1 us
    reshape x2, local copies, waits for them, and re-layouts, local(): arranged = grad_table.reshape(dom_count, edge_count * own_count, features)  31.3 us
    unnamed x62, local copies, waits for them, and re-layouts  23.8 us
  transfers between devices with their start and end apart: 8, of which 5 were waited for; matrix products, arithmetic and copies ran while one was open for 10% of the time, Pallas kernels for 0%

commit v1 on v0

v1 whole, which is shorter than its diff:
```python
import jax
import jax.numpy as jnp
from jax import lax
from jax.experimental import pallas as pl
from jax.experimental.pallas import tpu as pltpu
from jax.sharding import PartitionSpec as P

LEARN_RATE = 0.5
D = 400
HALF = 200
ROWS = 2048
EDGES = 512
NEG = 256
OWN_REL = 29
SLOT = 32
CUT = 208
Z = 8
BLOCKS = 32
MIB = 1 << 20
MESH = pl.DeviceIdType.MESH
BF = jnp.bfloat16
F32 = jnp.float32

GATHER_ORDER = (0, -1, 1, -2, 2, -3, 3, 4)
SCATTER_ORDER = (4, 3, -3, 2, -2, 1, -1, 0)


class Place:
    def __init__(self):
        self.d = lax.axis_index("dom")
        self.e = lax.axis_index("edge")
        self.y = lax.rem(self.d, 4)
        self.z = lax.rem(self.d // 4, Z)
        self.xl = self.d // 32
        self.xh = self.e // 2
        self.c = lax.rem(self.e, 2)
        x = self.xh * 2 + self.xl
        other = lax.rem(self.d + 32, 64)
        self.x_up = (other, (lax.rem(x + 1, 4) // 2) * 2 + self.c)
        self.x_down = (other, (lax.rem(x + 3, 4) // 2) * 2 + self.c)
        self.z_up = (self.xl * 32 + lax.rem(self.z + 1, Z) * 4 + self.y, self.e)
        self.z_down = (self.xl * 32 + lax.rem(self.z + 7, Z) * 4 + self.y, self.e)
        self.next = (lax.rem(self.d + 1, 64), self.e)
        self.prev = (lax.rem(self.d + 63, 64), self.e)
        self.sibling = (self.d, self.xh * 2 + 1 - self.c)
        self.far = (self.d, (1 - self.xh) * 2 + self.c)

    def group(self, y, e):
        return (self.d - self.y + y, e)

    def block(self, xl, offset, half):
        return (xl * Z + lax.rem(self.z + offset + Z, Z)) * 2 + half


def greet(at):
    barrier = pltpu.get_barrier_semaphore()
    where = at.y * 4 + at.e
    for k in range(1, 16):
        peer = lax.rem(where + k, 16)
        pl.semaphore_signal(
            barrier, inc=1, device_id=at.group(peer // 4, lax.rem(peer, 4)), device_id_type=MESH
        )
    for peer in (at.x_up, at.x_down, at.z_up, at.z_down, at.next, at.prev):
        pl.semaphore_signal(barrier, inc=1, device_id=peer, device_id_type=MESH)
    pl.semaphore_wait(barrier, 21)


def send(src, dst, send_sem, recv_sem, peer):
    pltpu.make_async_remote_copy(
        src_ref=src,
        dst_ref=dst,
        send_sem=send_sem,
        recv_sem=recv_sem,
        device_id=peer,
        device_id_type=MESH,
    ).start()


def settle(ref, sem):
    pltpu.make_async_copy(ref, ref, sem).wait()


NP = 2
PW = ROWS // 2 // NP


def gather_kernel(
    shard, own, table, upper, lower, gath, blk,
    a_send, a_recv, z_send, z_recv, x_send, x_recv, s_send, s_recv, p_send, p_recv, q_send, q_recv, own_sem,
):
    at = Place()
    greet(at)

    slot = lax.rem(at.y, 2) * 4 + at.e
    row = pl.multiple_of(slot * SLOT, SLOT)
    here = at.c == at.y // 2
    mine = gath.at[pl.ds(row, SLOT), :]
    for k in range(8):
        y, xh = lax.rem(at.y + k // 2, 4), lax.rem(at.xh + k % 2, 2)
        peer = at.group(y, xh * 2 + at.y // 2)
        if k == 0:
            @pl.when(here)
            def _():
                pltpu.make_async_copy(shard, mine, a_recv.at[slot]).start()

            @pl.when(jnp.logical_not(here))
            def _():
                send(shard, mine, a_send.at[0], a_recv.at[slot], peer)
        else:
            send(shard, mine, a_send.at[k], a_recv.at[slot], peer)

    for n in range(NP):
        cols = pl.ds(pl.multiple_of(at.c * (ROWS // 2) + n * PW, PW), PW)
        send(own.at[:, cols], upper.at[:, cols], p_send.at[0, n], p_recv.at[0, n], at.prev)
        send(own.at[:, cols], lower.at[:, cols], p_send.at[1, n], p_recv.at[1, n], at.next)

    for k in range(8):
        settle(gath.at[pl.ds(k * SLOT, SLOT), :], a_recv.at[k])
    blk[...] = gath[...].astype(F32).T[:D].astype(BF)
    first = at.block(at.xl, 0, at.c)
    keep = pltpu.make_async_copy(blk, table.at[first], own_sem)
    keep.start()

    top, low = pl.ds(0, CUT), pl.ds(CUT, D - CUT)

    def index(j, xl=None):
        return at.block(at.xl if xl is None else xl, GATHER_ORDER[j], at.c)

    def whole(j):
        return blk if j == 0 else table.at[index(j)]

    def along_x(j, part):
        rows, peer = ((top, at.x_up), (low, at.x_down))[part]
        src = blk.at[rows, :] if j == 0 else table.at[index(j), rows, :]
        send(src, table.at[index(j), rows, :], x_send.at[part, j], x_recv.at[part, j], peer)

    def to_sibling(j, xl=None):
        n = index(j, xl)
        q = j if xl is None else 8 + j
        src = blk if q == 0 else table.at[n]
        send(src, table.at[n], s_send.at[q], s_recv.at[q], at.sibling)

    def along_z(way, step):
        j = (0, 2 * step - 1 + way)[step > 0]
        peer = (at.z_up, at.z_down)[way]
        if step < 3:
            send(whole(j), table.at[index(j)], z_send.at[way, step], z_recv.at[way, step], peer)
        else:
            rows = (top, low)[way]
            ref = table.at[index(j), rows, :]
            send(ref, ref, z_send.at[way, step], z_recv.at[way, step], peer)

    def from_x(j):
        n = index(j, 1 - at.xl)
        settle(table.at[n, top, :], x_recv.at[0, j])
        settle(table.at[n, low, :], x_recv.at[1, j])
        to_sibling(j, 1 - at.xl)

    along_z(0, 0)
    along_z(1, 0)
    along_x(0, 0)
    along_x(0, 1)
    to_sibling(0)
    for step in range(3):
        for way in range(2):
            j = 2 * step + 1 + way
            settle(table.at[index(j)], z_recv.at[way, step])
            along_z(way, step + 1)
            along_x(j, 0)
            along_x(j, 1)
            to_sibling(j)
        if step == 0:
            from_x(0)
        else:
            from_x(2 * step - 1)
            from_x(2 * step)
    settle(table.at[index(7), top, :], z_recv.at[0, 3])
    along_x(7, 0)
    settle(table.at[index(7), low, :], z_recv.at[1, 3])
    along_x(7, 1)
    to_sibling(7)
    from_x(5)
    from_x(6)
    for n in range(NP):
        cols = pl.ds(pl.multiple_of(at.c * (ROWS // 2) + n * PW, PW), PW)
        for way, ref in enumerate((upper, lower)):
            part = ref.at[:, cols]
            settle(part, p_recv.at[way, n])
            send(part, part, q_send.at[way, n], q_recv.at[way, n], at.sibling)
    from_x(7)

    for j in range(8):
        settle(table.at[at.block(at.xl, GATHER_ORDER[j], 1 - at.c)], s_recv.at[j])
        settle(table.at[at.block(1 - at.xl, GATHER_ORDER[j], 1 - at.c)], s_recv.at[8 + j])
    for n in range(NP):
        cols = pl.ds(pl.multiple_of((1 - at.c) * (ROWS // 2) + n * PW, PW), PW)
        settle(upper.at[:, cols], q_recv.at[0, n])
        settle(lower.at[:, cols], q_recv.at[1, n])
    keep.wait()

    @pl.when(jnp.logical_not(here))
    def _():
        settle(shard, a_send.at[0])

    for k in range(1, 8):
        settle(shard, a_send.at[k])
    for way in range(2):
        for n in range(NP):
            settle(upper.at[:, pl.ds(0, PW)], p_send.at[way, n])
            settle(upper.at[:, pl.ds(0, PW)], q_send.at[way, n])
        for step in range(3):
            settle(blk, z_send.at[way, step])
        settle(blk.at[(top, low)[way], :], z_send.at[way, 3])
        for j in range(8):
            settle(blk.at[(top, low)[way], :], x_send.at[way, j])
    for q in range(16):
        settle(blk, s_send.at[q])


def gather_all(shard, own):
    dma = pltpu.SemaphoreType.DMA
    part = jax.ShapeDtypeStruct((D, ROWS), BF)
    anywhere = pl.BlockSpec(memory_space=pl.ANY)
    return pl.pallas_call(
        gather_kernel,
        out_shape=(jax.ShapeDtypeStruct((BLOCKS, D, 256), BF), part, part),
        in_specs=[pl.BlockSpec(memory_space=pltpu.VMEM), anywhere],
        out_specs=(anywhere, anywhere, anywhere),
        scratch_shapes=[
            pltpu.VMEM((256, 512), BF),
            pltpu.VMEM((D, 256), BF),
            dma((8,)), dma((8,)),
            dma((2, 4)), dma((2, 4)),
            dma((2, 8)), dma((2, 8)),
            dma((16,)), dma((16,)),
            dma((2, NP)), dma((2, NP)),
            dma((2, NP)), dma((2, NP)),
            dma,
        ],
        compiler_params=pltpu.CompilerParams(
            collective_id=0, has_side_effects=True, vmem_limit_bytes=16 * MIB
        ),
        name="gather_all",
    )(shard, own)


def onehot(ids, base, rows):
    at = lax.broadcasted_iota(jnp.int32, (rows, ids.shape[1]), 0) + base
    return jnp.where(at == ids, 1.0, 0.0).astype(BF)


def dot(a, b, over=((1,), (0,))):
    return lax.dot_general(a, b, (over, ((), ())), preferred_element_type=F32)


ACROSS = ((1,), (1,))


def compute_kernel(
    own, upper, lower, table, heads, tails, negs, rels,
    own_out, upper_out, lower_out, table_out,
    head_vec, part_vec, rel_vec, head_grad, part_grad, rel_grad,
):
    def fetch(source, ids, out, cols):
        out[:, cols] = dot(source[:, :1024], onehot(ids, 0, 1024)) + dot(
            source[:, 1024:], onehot(ids, 1024, 1024)
        )

    for b, source in enumerate((upper, lower)):
        fetch(own, heads[b:b + 1, :], head_vec, pl.ds(b * EDGES, EDGES))
        fetch(source, tails[b:b + 1, :], part_vec, pl.ds(b * 768, EDGES))
        fetch(source, negs[b:b + 1, :], part_vec, pl.ds(b * 768 + EDGES, NEG))

    rel_vec[...] = jnp.zeros_like(rel_vec)

    @pl.loop(0, BLOCKS // 4)
    def _(k):
        for b in range(2):
            ids = rels[b:b + 1, :]
            total = None
            for i in range(4):
                term = dot(table[k * 4 + i], onehot(ids, (k * 4 + i) * 256, 256))
                total = term if total is None else total + term
            rel_vec[:, b * EDGES:(b + 1) * EDGES] += total

    for b in range(2):
        span = slice(b * EDGES, (b + 1) * EDGES)
        h_re, h_im = head_vec[:HALF, span], head_vec[HALF:, span]
        r_re, r_im = rel_vec[:HALF, span], rel_vec[HALF:, span]
        q = jnp.concatenate([h_re * r_re - h_im * r_im, h_re * r_im + h_im * r_re], axis=0)
        q_low = q.astype(BF)
        tail = part_vec[:, b * 768:b * 768 + EDGES]
        cand = part_vec[:, b * 768 + EDGES:(b + 1) * 768].astype(BF)
        positive = jnp.sum(q * tail, axis=0, keepdims=True)
        slope = -jax.nn.sigmoid(-positive)
        scores = dot(cand, q_low, ((0,), (0,)))
        neg_slope = jax.nn.sigmoid(scores).astype(BF)
        u = slope * tail + dot(cand, neg_slope)
        part_grad[b, :, :EDGES] = (slope * q).astype(BF)
        part_grad[b, :, EDGES:] = dot(q_low, neg_slope, ACROSS).astype(BF)
        u_re, u_im = u[:HALF], u[HALF:]
        head_grad[:, span] = jnp.concatenate(
            [u_re * r_re + u_im * r_im, u_im * r_re - u_re * r_im], axis=0
        ).astype(BF)
        rel_grad[:, span] = jnp.concatenate(
            [u_re * h_re + u_im * h_im, u_im * h_re - u_re * h_im], axis=0
        ).astype(BF)

    @pl.loop(0, BLOCKS)
    def _(k):
        table_out[k] = (
            dot(rel_grad[:, :EDGES], onehot(rels[0:1, :], k * 256, 256), ACROSS)
            + dot(rel_grad[:, EDGES:], onehot(rels[1:2, :], k * 256, 256), ACROSS)
        ).astype(BF)

    @pl.loop(0, ROWS // 256)
    def _(k):
        cols = pl.ds(pl.multiple_of(k * 256, 256), 256)
        own_out[:, cols] = (
            dot(head_grad[:, :EDGES], onehot(heads[0:1, :], k * 256, 256), ACROSS)
            + dot(head_grad[:, EDGES:], onehot(heads[1:2, :], k * 256, 256), ACROSS)
        ).astype(BF)
        for b, out in enumerate((upper_out, lower_out)):
            out[:, cols] = (
                dot(part_grad[b, :, :EDGES], onehot(tails[b:b + 1, :], k * 256, 256), ACROSS)
                + dot(part_grad[b, :, EDGES:], onehot(negs[b:b + 1, :], k * 256, 256), ACROSS)
            ).astype(BF)


def compute(own, upper, lower, table, heads, tails, negs, rels):
    part = jax.ShapeDtypeStruct((D, ROWS), BF)
    vmem = pl.BlockSpec(memory_space=pltpu.VMEM)
    return pl.pallas_call(
        compute_kernel,
        out_shape=(part, part, part, jax.ShapeDtypeStruct((BLOCKS, D, 256), BF)),
        in_specs=[vmem] * 8,
        out_specs=(vmem,) * 4,
        scratch_shapes=[
            pltpu.VMEM((D, 2 * EDGES), F32),
            pltpu.VMEM((D, 1536), F32),
            pltpu.VMEM((D, 2 * EDGES), F32),
            pltpu.VMEM((D, 2 * EDGES), BF),
            pltpu.VMEM((2, D, 768), BF),
            pltpu.VMEM((D, 2 * EDGES), BF),
        ],
        compiler_params=pltpu.CompilerParams(vmem_limit_bytes=56 * MIB),
        name="compute",
    )(own, upper, lower, table, heads, tails, negs, rels)


NE = 4
EW = ROWS // 2 // NE


def scatter_kernel(
    grads, own, upper, lower, rel_out, ent_out,
    sib, xs, xbuf, zs, zbuf, esib, es, fr, ss, far, fin, parts,
    s_send, s_recv, x_send, x_recv, z_send, z_recv, e_send, e_recv, n_send, n_recv,
    f_send, f_recv, g_send, g_recv, c_send, c_recv,
):
    at = Place()
    greet(at)
    top, low = pl.ds(0, CUT), pl.ds(CUT, D - CUT)
    halves = (top, low)
    tables = (upper, lower, own)

    def index(q, half):
        xl = 1 - at.xl if q < 8 else at.xl
        return at.block(xl, SCATTER_ORDER[q % 8], half)

    def swap(q):
        send(grads.at[index(q, 1 - at.c)], sib.at[q], s_send.at[q], s_recv.at[q], at.sibling)

    def cols_of(half, k):
        return pl.ds(pl.multiple_of(half * (ROWS // 2) + k * EW, EW), EW)

    def swap_part(t, k):
        send(
            tables[t].at[:, cols_of(1 - at.c, k)], esib.at[t, k],
            e_send.at[t, k], e_recv.at[t, k], at.sibling,
        )

    for k in range(NE):
        swap_part(0, k)
        swap_part(1, k)
        swap(2 * k)
        swap(2 * k + 1)
    for k in range(NE):
        swap(8 + 2 * k)
        swap(9 + 2 * k)
        swap_part(2, k)

    def both(q):
        settle(sib.at[q], s_recv.at[q])
        return grads[index(q, at.c)].astype(F32) + sib[q].astype(F32)

    def part_sum(t, k):
        settle(esib.at[t, k], e_recv.at[t, k])
        return tables[t][:, cols_of(at.c, k)].astype(F32) + esib[t, k].astype(F32)

    for k in range(NE):
        for t, peer in ((0, at.next), (1, at.prev)):
            es[t, k] = part_sum(t, k).astype(BF)
            send(es.at[t, k], fr.at[t, k], n_send.at[t, k], n_recv.at[t, k], peer)
        for j in (2 * k, 2 * k + 1):
            xs[j] = both(j).astype(BF)
            for part, peer in ((0, at.x_up), (1, at.x_down)):
                send(
                    xs.at[j, halves[part], :], xbuf.at[j, halves[part], :],
                    x_send.at[part, j], x_recv.at[part, j], peer,
                )

    def along_x(j):
        total = both(8 + j)
        settle(xbuf.at[j, top, :], x_recv.at[0, j])
        settle(xbuf.at[j, low, :], x_recv.at[1, j])
        return total + xbuf[j].astype(F32)

    def z_step(step):
        if step == 0:
            zs[0] = along_x(0).astype(BF)
            for way, peer in ((0, at.z_up), (1, at.z_down)):
                send(
                    zs.at[0, halves[way], :], zbuf.at[way, 0, halves[way], :],
                    z_send.at[way, 0], z_recv.at[way, 0], peer,
                )
            return
        for way, peer in ((0, at.z_up), (1, at.z_down)):
            j = 2 * step - 1 + way
            total = along_x(j)
            if step == 1:
                settle(zbuf.at[way, 0, halves[way], :], z_recv.at[way, 0])
                zs[j] = total.astype(BF)
                start, size = ((0, CUT), (CUT, D - CUT))[way]
                zs[j, start:start + size, :] = (
                    total[start:start + size] + zbuf[way, 0, start:start + size, :].astype(F32)
                ).astype(BF)
            else:
                settle(zbuf.at[way, step - 1], z_recv.at[way, step - 1])
                zs[j] = (total + zbuf[way, step - 1].astype(F32)).astype(BF)
            send(zs.at[j], zbuf.at[way, step], z_send.at[way, step], z_recv.at[way, step], peer)

    def part_step(k):
        total = part_sum(2, k)
        settle(fr.at[0, k], n_recv.at[0, k])
        settle(fr.at[1, k], n_recv.at[1, k])
        ss[k] = (total + fr[0, k].astype(F32) + fr[1, k].astype(F32)).astype(BF)
        send(ss.at[k], far.at[k], f_send.at[k], f_recv.at[k], at.far)

    def part_end(k):
        settle(far.at[k], f_recv.at[k])
        ent_out[:, cols_of(at.c, k)] = (ss[k].astype(F32) + far[k].astype(F32)).astype(BF)
        ref = ent_out.at[:, cols_of(at.c, k)]
        send(ref, ref, g_send.at[k], g_recv.at[k], at.sibling)

    z_step(0)
    part_step(0)
    z_step(1)
    part_step(1)
    z_step(2)
    part_step(2)
    z_step(3)
    part_step(3)
    part_end(0)
    part_end(1)

    total = along_x(7)
    for way in range(2):
        settle(zbuf.at[way, 3], z_recv.at[way, 3])
    total = total + zbuf[0, 3].astype(F32) + zbuf[1, 3].astype(F32)
    fin[...] = jnp.concatenate([total, jnp.zeros((512 - D, 256), F32)], axis=0).T
    source = at.y * 2 + at.xh
    for k in range(8):
        y, e = 2 * at.c + k // 4, k % 4
        here = jnp.logical_and(at.y == y, at.e == e)
        piece = fin.at[pl.ds(k * SLOT, SLOT), :]

        @pl.when(here)
        def _():
            pltpu.make_async_copy(piece, parts.at[source], c_recv.at[source]).start()

        @pl.when(jnp.logical_not(here))
        def _():
            send(piece, parts.at[source], c_send.at[k], c_recv.at[source], at.group(y, e))

    part_end(2)
    part_end(3)
    for k in range(8):
        settle(parts.at[k], c_recv.at[k])
    rel_out[...] = jnp.sum(parts[...], axis=0)

    for k in range(NE):
        settle(ent_out.at[:, cols_of(1 - at.c, k)], g_recv.at[k])
    for k in range(8):
        y, e = 2 * at.c + k // 4, k % 4

        @pl.when(jnp.logical_not(jnp.logical_and(at.y == y, at.e == e)))
        def _():
            settle(parts.at[k], c_send.at[k])

    for q in range(16):
        settle(sib.at[q], s_send.at[q])
    for k in range(NE):
        for t in range(3):
            settle(esib.at[t, k], e_send.at[t, k])
        for t in range(2):
            settle(es.at[t, k], n_send.at[t, k])
        settle(ss.at[k], f_send.at[k])
        settle(ss.at[k], g_send.at[k])
    for way in range(2):
        for j in range(8):
            settle(xs.at[j, halves[way], :], x_send.at[way, j])
        settle(zs.at[0, halves[way], :], z_send.at[way, 0])
        for step in range(1, 4):
            settle(zs.at[0], z_send.at[way, step])


def scatter_all(grads, own, upper, lower):
    dma = pltpu.SemaphoreType.DMA
    vmem = pl.BlockSpec(memory_space=pltpu.VMEM)
    block = (D, 256)
    return pl.pallas_call(
        scatter_kernel,
        out_shape=(
            jax.ShapeDtypeStruct((SLOT, 512), F32),
            jax.ShapeDtypeStruct((D, ROWS), BF),
        ),
        in_specs=[vmem] * 4,
        out_specs=(vmem, vmem),
        scratch_shapes=[
            pltpu.VMEM((16,) + block, BF),
            pltpu.VMEM((8,) + block, BF),
            pltpu.VMEM((8,) + block, BF),
            pltpu.VMEM((7,) + block, BF),
            pltpu.VMEM((2, 4) + block, BF),
            pltpu.VMEM((3, NE, D, EW), BF),
            pltpu.VMEM((2, NE, D, EW), BF),
            pltpu.VMEM((2, NE, D, EW), BF),
            pltpu.VMEM((NE, D, EW), BF),
            pltpu.VMEM((NE, D, EW), BF),
            pltpu.VMEM((256, 512), F32),
            pltpu.VMEM((8, SLOT, 512), F32),
            dma((16,)), dma((16,)),
            dma((2, 8)), dma((2, 8)),
            dma((2, 4)), dma((2, 4)),
            dma((3, NE)), dma((3, NE)),
            dma((2, NE)), dma((2, NE)),
            dma((NE,)), dma((NE,)),
            dma((NE,)), dma((NE,)),
            dma((8,)), dma((8,)),
        ],
        compiler_params=pltpu.CompilerParams(
            collective_id=1, has_side_effects=True, vmem_limit_bytes=56 * MIB
        ),
        name="scatter_all",
    )(grads, own, upper, lower)


def local(
    entity_emb,
    entity_state,
    relation_emb,
    relation_state,
    head_rows,
    tail_rows,
    relation_ids,
    negative_rows,
):
    entity = entity_emb.T
    own = entity.astype(BF)
    shard = jnp.pad(relation_emb.astype(BF), ((0, SLOT - OWN_REL), (0, 512 - D)))
    rels = relation_ids // OWN_REL * SLOT + relation_ids % OWN_REL
    table, upper, lower = gather_all(shard, own)
    own_part, upper_part, lower_part, grads = compute(
        own, upper, lower, table, head_rows, tail_rows, negative_rows[:, 0], rels
    )
    relation_grad, entity_grad = scatter_all(grads, own_part, upper_part, lower_part)

    entity_grad = entity_grad.astype(F32)
    new_entity_state = entity_state + jnp.mean(entity_grad * entity_grad, axis=0)
    new_entity = entity - LEARN_RATE * entity_grad / jnp.sqrt(new_entity_state)
    relation_grad = relation_grad[:OWN_REL, :D]
    new_relation_state = relation_state + jnp.mean(relation_grad * relation_grad, axis=-1)
    new_relation_emb = relation_emb - LEARN_RATE * relation_grad / jnp.sqrt(new_relation_state)[:, None]
    return (new_entity.T, new_entity_state, new_relation_emb, new_relation_state)


def solution(mesh):
    placed = (
        P("dom", None),
        P("dom"),
        P(("dom", "edge"), None),
        P(("dom", "edge")),
        P(None, ("dom", "edge")),
        P(None, ("dom", "edge")),
        P(None, ("dom", "edge")),
        P(None, ("dom", "edge"), None),
    )
    return jax.shard_map(
        local,
        mesh=mesh,
        in_specs=placed,
        out_specs=(P("dom", None), P("dom"), P(("dom", "edge"), None), P(("dom", "edge"))),
        check_vma=False,
    )
```

time: 1040 us -> 199 us (0.19); the launches traced: 1020 us -> 197 us
  waiting for transfers between devices: 776 us -> 0 us
  Pallas kernels: 0 us -> 176 us
  local copies, waits for them, and re-layouts: 110 us -> 6.32 us
  other arithmetic: 80.3 us -> 13.6 us
  starting transfers between devices: 28.5 us -> 0 us
  between operations: 15.5 us -> 0.71 us
    all_gather x1 -> x0, waiting for transfers between devices: 384 us -> none  [local(): lax.all_gather(relation_emb.astype(jnp.bfloat16), ('dom', 'edge'), axis=0...]
    ppermute x4 -> x0, waiting for transfers between devices: 304 us -> none  [shifted(): return lax.ppermute(value, axis, pairs)]
    pallas_call x0 -> x3, Pallas kernels: none -> 176 us  [the longest x1 76.5 us: scatter_all(): pl.pallas_call(scatter_kernel, out_shape=(jax.ShapeDtypeStruct((SLOT, 512...]
    psum x1 -> x0, waiting for transfers between devices: 88.1 us -> none  [local(): entity_grad = lax.psum(local_total, 'edge')]
    scatter-add x5 -> x0, other arithmetic: 38.2 us -> none  [the longest x1 13.6 us: local(): jnp.zeros((rel_total, features), jnp.float32).at[all_ids].add(all_grads)]
    reshape x2 -> x0, local copies, waits for them, and re-layouts: 31.3 us -> none  [local(): arranged = grad_table.reshape(dom_count, edge_count * own_count, features)]
    gather x14 -> x0, local copies, waits for them, and re-layouts: 30.4 us -> none  [the longest x4 13.9 us: bucket_terms(): rel_vec = relation_table[relation_index].astype(jnp.float32)]
    unnamed x62 -> x17, local copies, waits for them, and re-layouts: 23.8 us -> 6.31 us
  transfers between devices with their start and end apart: 8 -> 0, of which waited for: 5 -> 0; matrix products, arithmetic and copies ran while one was open for 10% -> 0% of each run, Pallas kernels for 0% -> 0%
where the time goes in v1:
time: 199 us; the launch traced here: 197 us
  Pallas kernels  176 us (88%)
  other arithmetic  13.6 us (7%)
  local copies, waits for them, and re-layouts  6.32 us (3%)
    pallas_call x1, Pallas kernels, scatter_all(): pl.pallas_call(scatter_kernel, out_shape=(jax.ShapeDtypeStruct((SLOT, 512...  76.5 us
    pallas_call x1, Pallas kernels, gather_all(): pl.pallas_call(gather_kernel, out_shape=(jax.ShapeDtypeStruct((BLOCKS, D,...  58 us
    pallas_call x1, Pallas kernels, compute(): pl.pallas_call(compute_kernel, out_shape=(part, part, part, jax.ShapeDtyp...  42 us
    unnamed x17, local copies, waits for them, and re-layouts  6.31 us

profile of v1, /device:TPU:1, one launch (start us, length us, event | category | flops | bytes accessed | tf_op | source)
XLA Modules:
  0.0 197.1 jit_solution(17467958096537522056)
XLA Ops:
  0.6 1.3 copy.14
  1.9 1.3 fusion.4.rels
  3.2 0.8 convert_element_type.12
  4.0 2.2 %bitcast_convert_fusion.own = bf16[400,2048]{1,0:T(8,128)(2,1)S(1)} fusion(f32[2048,400]{0,1:T(8,128)} %param.8), kind=kLoop, calls=%fused_computation.6 | loop fusion | flops 819200 | bytes 4915200 | tf_op jit(solution)/shard_map/convert_element_type | solution.py:570
  6.2 0.0 copy-start
  6.2 58.0 %gather_all.1 = (bf16[32,400,256]{2,1,0:T(8,128)(2,1)S(1)}, bf16[400,2048]{1,0:T(8,128)(2,1)S(1)}, bf16[400,2048]{1,0:T(8,128)(2,1)S(1)}) custom-call(bf16[32,512]{1,0:T(8,128)(2,1)S(1)} %pad.4.shard, bf16[400,2048]{1,0:T(8,128)(2,1)S(1)} %bitcast_convert_fusion.own), custom_call_target="tpu_custom_call" | custom-call | tf_op jit(solution)/shard_map/gather_all/pallas_call | solution.py:224
  64.2 0.0 copy-start.1
  64.2 2.7 %copy-done.1 = bf16[32,400,256]{2,1,0:T(8,128)(2,1)} copy-done((bf16[32,400,256]{2,1,0:T(8,128)(2,1)}, bf16[32,400,256]{2,1,0:T(8,128)(2,1)S(1)}, u32[]{:S(2)}) %copy-start.1) | copy-done | bytes 6553624
  66.9 0.0 copy-start.2
  67.0 1.2 copy-done.2
  68.1 0.0 copy-start.3
  68.1 1.2 copy-done.3
  69.3 0.0 copy-done
  69.3 42.0 %compute.1 = (bf16[400,2048]{1,0:T(8,128)(2,1)}, bf16[400,2048]{1,0:T(8,128)(2,1)}, bf16[400,2048]{1,0:T(8,128)(2,1)}, bf16[32,400,256]{2,1,0:T(8,128)(2,1)}) custom-call(bf16[400,2048]{1,0:T(8,128)(2,1)} %copy-done, bf16[400,2048]{1,0:T(8,128)(2,1)} %copy-done.2, bf16[400,2048]{1,0:T(8,128)(2,1)} %copy-done.3, bf16[32,400,256]{2,1,0:T(8,128)(2,1)} %copy-done.1, ...), custom_call_target="tpu_custom_call" | custom-call | tf_op jit(solution)/shard_map/compute/pallas_call | solution.py:333
  111.2 0.0 copy-start.7
  111.2 0.0 copy-start.5
  111.2 0.0 copy-start.6
  111.3 0.0 copy-start.4
  111.3 76.5 %scatter_all.1 = (f32[32,512]{1,0:T(8,128)}, bf16[400,2048]{1,0:T(8,128)(2,1)}) custom-call(bf16[32,400,256]{2,1,0:T(8,128)(2,1)} %get-tuple-element.16.grads, bf16[400,2048]{1,0:T(8,128)(2,1)} %get-tuple-element.17.own, bf16[400,2048]{1,0:T(8,128)(2,1)} %get-tuple-element.18.upper, bf16[400,2048]{1,0:T(8,128)(2,1)} %get-tuple-element.19.lower), custom_call_target="tpu_custom_call" | custom-call | tf_op jit(solution)/shard_map/scatter_all/pallas_call | solution.py:522
  187.8 1.0 multiply_reduce_fusion
  188.7 0.0 copy-done.7
  188.7 0.5 fusion.5
  189.3 0.0 copy-done.5
  189.3 1.5 divide_subtract_fusion
  190.8 1.8 fusion.3
  192.6 0.0 copy-done.6
  192.6 0.6 fusion.6
  193.2 0.0 copy-done.4
  193.2 3.9 %fusion.2 = f32[2048,400]{0,1:T(8,128)} fusion(bf16[400,2048]{1,0:T(8,128)(2,1)} %get-tuple-element.20, f32[2048,400]{0,1:T(8,128)S(1)} %copy-done.4, f32[2048]{0:T(1024)S(1)} %get-tuple-element.24), kind=kLoop, calls=%fused_computation.4 | loop fusion | flops 3276800 | bytes 8200192 | tf_op jit(solution)/shard_map/transpose | solution.py:585
  (1 shorter events, 0.0 us)
Async XLA Ops:
  6.2 63.1 %copy-start = (bf16[400,2048]{1,0:T(8,128)(2,1)}, bf16[400,2048]{1,0:T(8,128)(2,1)S(1)}, u32[]{:S(2)}) copy-start(bf16[400,2048]{1,0:T(8,128)(2,1)S(1)} %bitcast_convert_fusion.own) | copy-start | bytes 4915204
  64.2 2.7 %copy-start.1 = (bf16[32,400,256]{2,1,0:T(8,128)(2,1)}, bf16[32,400,256]{2,1,0:T(8,128)(2,1)S(1)}, u32[]{:S(2)}) copy-start(bf16[32,400,256]{2,1,0:T(8,128)(2,1)S(1)} %get-tuple-element.15.table) | copy-start | bytes 19660804
  66.9 1.2 copy-start.2
  68.1 1.2 copy-start.3
  111.2 77.5 %copy-start.7 = (f32[29]{0:T(128)S(1)}, f32[29]{0:T(128)}, u32[]{:S(2)}) copy-start(f32[29]{0:T(128)} %param.11) | copy-start | bytes 352
  111.2 78.0 %copy-start.5 = (f32[29,400]{1,0:T(8,128)S(1)}, f32[29,400]{1,0:T(8,128)}, u32[]{:S(2)}) copy-start(f32[29,400]{1,0:T(8,128)} %param.10) | copy-start | bytes 139204
  111.2 81.3 %copy-start.6 = (f32[2048]{0:T(1024)S(1)}, f32[2048]{0:T(1024)}, u32[]{:S(2)}) copy-start(f32[2048]{0:T(1024)} %param.9) | copy-start | bytes 24580
  111.3 81.9 %copy-start.4 = (f32[2048,400]{0,1:T(8,128)S(1)}, f32[2048,400]{0,1:T(8,128)}, u32[]{:S(2)}) copy-start(f32[2048,400]{0,1:T(8,128)} %param.8) | copy-start | bytes 9830404

commit v2 on v0

v2 whole, which is shorter than its diff:
```python
import jax
import jax.numpy as jnp
from jax import lax
from jax.experimental import pallas as pl
from jax.experimental.pallas import tpu as pltpu
from jax.sharding import PartitionSpec as P

LEARN_RATE = 0.5
D = 400
HALF = 200
ROWS = 2048
EDGES = 512
NEG = 256
PICKS = EDGES + NEG
OWN_REL = 29
SLOT = 32
CUT = 208
Z = 8
BLOCKS = 32
MIB = 1 << 20
MESH = pl.DeviceIdType.MESH
BF = jnp.bfloat16
F32 = jnp.float32
ACROSS = ((1,), (1,))


class Place:
    def __init__(self):
        self.d = lax.axis_index("dom")
        self.e = lax.axis_index("edge")
        self.y = lax.rem(self.d, 4)
        self.z = lax.rem(self.d // 4, Z)
        self.xl = self.d // 32
        self.xh = self.e // 2
        self.c = lax.rem(self.e, 2)
        x = self.xh * 2 + self.xl
        other = lax.rem(self.d + 32, 64)
        self.x_up = (other, (lax.rem(x + 1, 4) // 2) * 2 + self.c)
        self.x_down = (other, (lax.rem(x + 3, 4) // 2) * 2 + self.c)
        self.z_up = self.along_z(0)
        self.z_down = self.along_z(1)
        self.next = (lax.rem(self.d + 1, 64), self.e)
        self.prev = (lax.rem(self.d + 63, 64), self.e)
        self.sibling = (self.d, self.xh * 2 + 1 - self.c)
        self.far = (self.d, (1 - self.xh) * 2 + self.c)

    def along_z(self, way):
        return (self.xl * 32 + lax.rem(self.z + 1 + 6 * way, Z) * 4 + self.y, self.e)

    def group(self, y, e):
        return (self.d - self.y + y, e)

    def block(self, xl, offset, half):
        return (xl * Z + lax.rem(self.z + offset + Z, Z)) * 2 + half

    def incoming(self, j, xl, half):
        return self.block(xl, jnp.where(j % 2 == 1, -((j + 1) // 2), j // 2), half)

    def outgoing(self, j, xl, half):
        away = 4 - (j + 1) // 2
        return self.block(xl, jnp.where(j % 2 == 1, away, -away), half)


def greet(at):
    barrier = pltpu.get_barrier_semaphore()
    where = at.y * 4 + at.e
    for k in range(1, 16):
        peer = lax.rem(where + k, 16)
        pl.semaphore_signal(
            barrier, inc=1, device_id=at.group(peer // 4, lax.rem(peer, 4)), device_id_type=MESH
        )
    for peer in (at.x_up, at.x_down, at.z_up, at.z_down, at.next, at.prev):
        pl.semaphore_signal(barrier, inc=1, device_id=peer, device_id_type=MESH)
    pl.semaphore_wait(barrier, 21)


def send(src, dst, send_sem, recv_sem, peer):
    pltpu.make_async_remote_copy(
        src_ref=src,
        dst_ref=dst,
        send_sem=send_sem,
        recv_sem=recv_sem,
        device_id=peer,
        device_id_type=MESH,
    ).start()


def settle(ref, sem):
    pltpu.make_async_copy(ref, ref, sem).wait()


def onehot(ids, base, rows):
    at = lax.broadcasted_iota(jnp.int32, (rows, ids.shape[1]), 0) + base
    return jnp.where(at == ids, 1.0, 0.0).astype(BF)


def dot(a, b, over=((1,), (0,))):
    return lax.dot_general(a, b, (over, ((), ())), preferred_element_type=F32)


def lanes(k):
    return pl.ds(pl.multiple_of(k * 256, 256), 256)


BLOCK = (D, 256)
DMA = pltpu.SemaphoreType.DMA
BUFFERS = (
    ("pad", (SLOT, 512), F32),
    ("shard", (SLOT, 512), BF),
    ("own", (D, ROWS), BF),
    ("rels", (2, EDGES), jnp.int32),
    ("ids_out", (2, 8, PICKS), jnp.int32),
    ("ids", (2, 8, PICKS), jnp.int32),
    ("gath", (256, 512), BF),
    ("table", (BLOCKS,) + BLOCK, BF),
    ("served", (2, 3) + BLOCK, BF),
    ("picked", (2, 3) + BLOCK, BF),
    ("head_vec", (D, 2 * EDGES), F32),
    ("rel_vec", (D, 2 * EDGES), F32),
    ("head_grad", (D, 2 * EDGES), BF),
    ("rel_grad", (D, 2 * EDGES), BF),
    ("pick_grad", (2, 3) + BLOCK, BF),
    ("pick_in", (2, 3) + BLOCK, BF),
    ("stage", (16,) + BLOCK, BF),
    ("sib", (16,) + BLOCK, BF),
    ("xs", (8,) + BLOCK, BF),
    ("xbuf", (8,) + BLOCK, BF),
    ("acc", BLOCK, F32),
    ("zs", (7,) + BLOCK, BF),
    ("zbuf", (2, 4) + BLOCK, BF),
    ("head_sum", (8,) + BLOCK, F32),
    ("ent_stage", (4,) + BLOCK, BF),
    ("ent_sib", (4,) + BLOCK, BF),
    ("ent_sum", (4,) + BLOCK, BF),
    ("ent_far", (4,) + BLOCK, BF),
    ("ent_end", (8,) + BLOCK, BF),
    ("fin", (256, 512), F32),
    ("parts", (8, SLOT, 512), F32),
)
SEMAPHORES = (
    ("a", (8,)), ("i", (2,)), ("p", (2, 3)), ("z", (2, 4)), ("x", (2, 8)), ("s", (16,)),
    ("n", (2, 3)), ("t", (16,)), ("w", (2, 8)), ("v", (2, 4)),
    ("es", (4,)), ("ef", (4,)), ("ee", (4,)), ("c", (8,)),
)


class Held:
    pass


def step_kernel(entity, relation, heads, tails, negs, relation_ids, rel_out, ent_out, *scratch):
    m = Held()
    names = [name for name, _, _ in BUFFERS]
    for name, _ in SEMAPHORES:
        names += [name + "_send", name + "_recv"]
    for name, ref in zip(names, scratch, strict=True):
        setattr(m, name, ref)
    at = Place()
    top, low = pl.ds(0, CUT), pl.ds(CUT, D - CUT)
    halves = (top, low)

    m.own[...] = entity[...].astype(BF)
    m.pad[...] = jnp.zeros_like(m.pad)
    m.pad[:OWN_REL, :D] = relation[...]
    m.shard[...] = m.pad[...].astype(BF)
    for b in range(2):
        m.ids_out[b, :, :EDGES] = jnp.broadcast_to(tails[b:b + 1, :], (8, EDGES))
        m.ids_out[b, :, EDGES:] = jnp.broadcast_to(negs[b], (8, NEG))
    ids = relation_ids[...]
    m.rels[...] = ids + (SLOT - OWN_REL) * ((ids * 36158) >> 20)
    greet(at)

    slot = lax.rem(at.y, 2) * 4 + at.e
    here = at.c == at.y // 2
    mine = m.gath.at[pl.ds(pl.multiple_of(slot * SLOT, SLOT), SLOT), :]
    for k in range(8):
        y, xh = lax.rem(at.y + k // 2, 4), lax.rem(at.xh + k % 2, 2)
        peer = at.group(y, xh * 2 + at.y // 2)
        if k == 0:
            @pl.when(here)
            def _():
                pltpu.make_async_copy(m.shard, mine, m.a_recv.at[slot]).start()

            @pl.when(jnp.logical_not(here))
            def _():
                send(m.shard, mine, m.a_send.at[0], m.a_recv.at[slot], peer)
        else:
            send(m.shard, mine, m.a_send.at[k], m.a_recv.at[slot], peer)
    for b, peer in enumerate((at.next, at.prev)):
        send(m.ids_out.at[b], m.ids.at[b], m.i_send.at[b], m.i_recv.at[b], peer)

    for k in range(8):
        settle(m.gath.at[pl.ds(k * SLOT, SLOT), :], m.a_recv.at[k])
    m.table[at.block(at.xl, 0, at.c)] = m.gath[...].astype(F32).T[:D].astype(BF)

    def along_z(j, way, step):
        ref = m.table.at[at.incoming(j, at.xl, at.c)]
        send(ref, ref, m.z_send.at[way, step], m.z_recv.at[way, step], at.along_z(way))

    def half_along_z(j, way):
        ref = m.table.at[at.incoming(j, at.xl, at.c), halves[way], :]
        send(ref, ref, m.z_send.at[way, 3], m.z_recv.at[way, 3], at.along_z(way))

    def along_x(j):
        for way, peer in ((0, at.x_up), (1, at.x_down)):
            ref = m.table.at[at.incoming(j, at.xl, at.c), halves[way], :]
            send(ref, ref, m.x_send.at[way, j], m.x_recv.at[way, j], peer)

    def to_sibling(j, xl, q):
        ref = m.table.at[at.incoming(j, xl, at.c)]
        send(ref, ref, m.s_send.at[q], m.s_recv.at[q], at.sibling)

    along_z(0, 0, 0)
    along_z(0, 1, 0)
    along_x(0)
    to_sibling(0, at.xl, 0)

    for b in range(2):
        settle(m.ids.at[b], m.i_recv.at[b])

    @pl.loop(0, 6)
    def _(t):
        b, n = t // 3, t % 3
        m.served[b, n] = dot(m.own[...], onehot(m.ids[b, 0:1, lanes(n)], 0, ROWS)).astype(BF)
        send(
            m.served.at[b, n], m.picked.at[b, n], m.p_send.at[b, n], m.p_recv.at[b, n],
            (lax.rem(at.d + 63 + 2 * b, 64), at.e),
        )

    m.rel_vec[...] = jnp.zeros_like(m.rel_vec)

    def head_rows(t):
        m.head_vec[:, lanes(t)] = dot(
            m.own[...], onehot(heads[pl.ds(t // 2, 1), lanes(t % 2)], 0, ROWS)
        )

    @pl.loop(1, 10)
    def _(j):
        way = (j + 1) % 2

        @pl.when(j <= 6)
        def _():
            settle(m.table.at[at.incoming(j, at.xl, at.c)], m.z_recv.at[way, (j - 1) // 2])

        @pl.when(j == 7)
        def _():
            for side in range(2):
                settle(m.table.at[at.incoming(j, at.xl, at.c), halves[side], :], m.z_recv.at[side, 3])

        @pl.when(j <= 4)
        def _():
            along_z(j, way, (j + 1) // 2)

        @pl.when(j == 5)
        def _():
            half_along_z(j, 0)

        @pl.when(j == 6)
        def _():
            half_along_z(j, 1)

        @pl.when(j <= 7)
        def _():
            along_x(j)
            to_sibling(j, at.xl, j)

        @pl.when(j <= 8)
        def _():
            for side in range(2):
                settle(
                    m.table.at[at.incoming(j - 1, 1 - at.xl, at.c), halves[side], :],
                    m.x_recv.at[side, j - 1],
                )
            to_sibling(j - 1, 1 - at.xl, 7 + j)

        @pl.when(j <= 4)
        def _():
            head_rows(j - 1)

        @pl.when(j >= 2)
        def _():
            k = j - 2
            for xl, q in ((at.xl, k), (1 - at.xl, 8 + k)):
                settle(m.table.at[at.incoming(k, xl, 1 - at.c)], m.s_recv.at[q])
            for b in range(2):
                total = None
                for xl in range(2):
                    for half in range(2):
                        n = at.incoming(k, xl, half)
                        term = dot(m.table[n], onehot(m.rels[b:b + 1, :], n * 256, 256))
                        total = term if total is None else total + term
                m.rel_vec[:, b * EDGES:(b + 1) * EDGES] += total

    for b in range(2):
        for n in range(3):
            settle(m.picked.at[b, n], m.p_recv.at[b, n])
        span = slice(b * EDGES, (b + 1) * EDGES)
        h_re, h_im = m.head_vec[:HALF, span], m.head_vec[HALF:, span]
        r_re, r_im = m.rel_vec[:HALF, span], m.rel_vec[HALF:, span]
        q = jnp.concatenate([h_re * r_re - h_im * r_im, h_re * r_im + h_im * r_re], axis=0)
        q_low = q.astype(BF)
        tail = jnp.concatenate([m.picked[b, 0], m.picked[b, 1]], axis=1).astype(F32)
        cand = m.picked[b, 2]
        positive = jnp.sum(q * tail, axis=0, keepdims=True)
        slope = -jax.nn.sigmoid(-positive)
        scores = dot(cand, q_low, ((0,), (0,)))
        neg_slope = jax.nn.sigmoid(scores).astype(BF)
        tail_grad = (slope * q).astype(BF)
        m.pick_grad[b, 0] = tail_grad[:, :256]
        m.pick_grad[b, 1] = tail_grad[:, 256:]
        m.pick_grad[b, 2] = dot(q_low, neg_slope, ACROSS).astype(BF)
        for n in range(3):
            send(
                m.pick_grad.at[b, n], m.pick_in.at[b, n], m.n_send.at[b, n], m.n_recv.at[b, n],
                (at.next, at.prev)[b],
            )
        u = slope * tail + dot(cand, neg_slope)
        u_re, u_im = u[:HALF], u[HALF:]
        m.rel_grad[:, span] = jnp.concatenate(
            [u_re * h_re + u_im * h_im, u_im * h_re - u_re * h_im], axis=0
        ).astype(BF)
        m.head_grad[:, span] = jnp.concatenate(
            [u_re * r_re + u_im * r_im, u_im * r_re - u_re * r_im], axis=0
        ).astype(BF)

    def rel_block(n):
        return dot(
            m.rel_grad[:, :EDGES], onehot(m.rels[0:1, :], n * 256, 256), ACROSS
        ) + dot(m.rel_grad[:, EDGES:], onehot(m.rels[1:2, :], n * 256, 256), ACROSS)

    def swap(j, xl, q):
        m.stage[q] = rel_block(at.outgoing(j, xl, 1 - at.c)).astype(BF)
        send(m.stage.at[q], m.sib.at[q], m.t_send.at[q], m.t_recv.at[q], at.sibling)

    @pl.loop(0, 9)
    def _(j):
        @pl.when(j < 8)
        def _():
            swap(j, 1 - at.xl, j)

        @pl.when(j > 0)
        def _():
            k = j - 1
            total = rel_block(at.outgoing(k, 1 - at.xl, at.c))
            settle(m.sib.at[k], m.t_recv.at[k])
            m.xs[k] = (total + m.sib[k].astype(F32)).astype(BF)
            for side, peer in ((0, at.x_up), (1, at.x_down)):
                send(
                    m.xs.at[k, halves[side], :], m.xbuf.at[k, halves[side], :],
                    m.w_send.at[side, k], m.w_recv.at[side, k], peer,
                )

    @pl.loop(0, 8)
    def _(j):
        swap(j, at.xl, 8 + j)

    def head_part(n):
        m.head_sum[n] = dot(
            m.head_grad[:, :EDGES], onehot(heads[0:1, :], n * 256, 256), ACROSS
        ) + dot(m.head_grad[:, EDGES:], onehot(heads[1:2, :], n * 256, 256), ACROSS)

    def entity_block(n):
        total = m.head_sum[n]
        for b in range(2):
            for i in range(3):
                ids = m.ids[b, 0:1, i * 256:(i + 1) * 256]
                total = total + dot(m.pick_in[b, i], onehot(ids, n * 256, 256), ACROSS)
        return total

    def entity_swap(k):
        m.ent_stage[k] = entity_block((1 - at.c) * 4 + k).astype(BF)
        send(m.ent_stage.at[k], m.ent_sib.at[k], m.es_send.at[k], m.es_recv.at[k], at.sibling)

    def entity_far(k):
        total = entity_block(at.c * 4 + k)
        settle(m.ent_sib.at[k], m.es_recv.at[k])
        m.ent_sum[k] = (total + m.ent_sib[k].astype(F32)).astype(BF)
        send(m.ent_sum.at[k], m.ent_far.at[k], m.ef_send.at[k], m.ef_recv.at[k], at.far)

    @pl.loop(0, 8)
    def _(j):
        total = rel_block(at.outgoing(j, at.xl, at.c))
        settle(m.sib.at[8 + j], m.t_recv.at[8 + j])
        for side in range(2):
            settle(m.xbuf.at[j, halves[side], :], m.w_recv.at[side, j])
        m.acc[...] = total + m.sib[8 + j].astype(F32) + m.xbuf[j].astype(F32)
        way, step = (j + 1) % 2, (j + 1) // 2

        for side in range(2):
            @pl.when(j == side + 1)
            def _():
                settle(m.zbuf.at[side, 0, halves[side], :], m.v_recv.at[side, 0])
                rows = (slice(0, CUT), slice(CUT, D))[side]
                m.acc[rows, :] += m.zbuf[side, 0, rows, :].astype(F32)

        @pl.when(jnp.logical_and(j >= 3, j <= 6))
        def _():
            settle(m.zbuf.at[way, step - 1], m.v_recv.at[way, step - 1])
            m.acc[...] += m.zbuf[way, step - 1].astype(F32)

        @pl.when(j == 0)
        def _():
            m.zs[0] = m.acc[...].astype(BF)
            for side in range(2):
                send(
                    m.zs.at[0, halves[side], :], m.zbuf.at[side, 0, halves[side], :],
                    m.v_send.at[side, 0], m.v_recv.at[side, 0], at.along_z(side),
                )

        @pl.when(jnp.logical_and(j >= 1, j <= 6))
        def _():
            m.zs[j] = m.acc[...].astype(BF)
            send(
                m.zs.at[j], m.zbuf.at[way, step], m.v_send.at[way, step], m.v_recv.at[way, step],
                at.along_z(way),
            )

        @pl.when(j < 4)
        def _():
            head_part(2 * j)
            head_part(2 * j + 1)

        @pl.when(j == 4)
        def _():
            for b in range(2):
                for n in range(3):
                    settle(m.pick_in.at[b, n], m.n_recv.at[b, n])

        @pl.when(jnp.logical_or(j == 4, j == 5))
        def _():
            @pl.loop(0, 2)
            def _(i):
                entity_swap(2 * (j - 4) + i)

        @pl.when(j >= 6)
        def _():
            @pl.loop(0, 2)
            def _(i):
                entity_far(2 * (j - 6) + i)

    for side in range(2):
        settle(m.zbuf.at[side, 3], m.v_recv.at[side, 3])
    total = m.acc[...] + m.zbuf[0, 3].astype(F32) + m.zbuf[1, 3].astype(F32)
    m.fin[...] = jnp.concatenate([total, jnp.zeros((512 - D, 256), F32)], axis=0).T
    source = at.y * 2 + at.xh
    for k in range(8):
        y, e = 2 * at.c + k // 4, k % 4
        mine_too = jnp.logical_and(at.y == y, at.e == e)
        piece = m.fin.at[pl.ds(k * SLOT, SLOT), :]

        @pl.when(mine_too)
        def _():
            pltpu.make_async_copy(piece, m.parts.at[source], m.c_recv.at[source]).start()

        @pl.when(jnp.logical_not(mine_too))
        def _():
            send(piece, m.parts.at[source], m.c_send.at[k], m.c_recv.at[source], at.group(y, e))

    @pl.loop(0, 4)
    def _(k):
        settle(m.ent_far.at[k], m.ef_recv.at[k])
        n = at.c * 4 + k
        m.ent_end[n] = (m.ent_sum[k].astype(F32) + m.ent_far[k].astype(F32)).astype(BF)
        send(m.ent_end.at[n], m.ent_end.at[n], m.ee_send.at[k], m.ee_recv.at[k], at.sibling)

    for k in range(8):
        settle(m.parts.at[k], m.c_recv.at[k])
    rel_out[...] = jnp.sum(m.parts[...], axis=0)
    for k in range(4):
        settle(m.ent_end.at[(1 - at.c) * 4 + k], m.ee_recv.at[k])
    for n in range(8):
        ent_out[:, n * 256:(n + 1) * 256] = m.ent_end[n]

    @pl.when(jnp.logical_not(here))
    def _():
        settle(m.shard, m.a_send.at[0])

    for k in range(1, 8):
        settle(m.shard, m.a_send.at[k])
    for k in range(8):
        y, e = 2 * at.c + k // 4, k % 4

        @pl.when(jnp.logical_not(jnp.logical_and(at.y == y, at.e == e)))
        def _():
            settle(m.parts.at[0], m.c_send.at[k])

    one = m.stage.at[0]
    for b in range(2):
        settle(m.ids_out.at[b], m.i_send.at[b])
        for n in range(3):
            settle(one, m.p_send.at[b, n])
            settle(one, m.n_send.at[b, n])
        half = m.stage.at[0, halves[b], :]
        for step in range(3):
            settle(one, m.z_send.at[b, step])
            settle(one, m.v_send.at[b, step + 1])
        settle(half, m.z_send.at[b, 3])
        settle(half, m.v_send.at[b, 0])
        for j in range(8):
            settle(half, m.x_send.at[b, j])
            settle(half, m.w_send.at[b, j])
    for q in range(16):
        settle(one, m.s_send.at[q])
        settle(one, m.t_send.at[q])
    for k in range(4):
        settle(one, m.es_send.at[k])
        settle(one, m.ef_send.at[k])
        settle(one, m.ee_send.at[k])


def whole_step(entity, relation, heads, tails, negs, relation_ids):
    vmem = pl.BlockSpec(memory_space=pltpu.VMEM)
    scratch = [pltpu.VMEM(shape, kind) for _, shape, kind in BUFFERS]
    for _, shape in SEMAPHORES:
        scratch += [DMA(shape), DMA(shape)]
    return pl.pallas_call(
        step_kernel,
        out_shape=(
            jax.ShapeDtypeStruct((SLOT, 512), F32),
            jax.ShapeDtypeStruct((D, ROWS), BF),
        ),
        in_specs=[vmem] * 6,
        out_specs=(vmem, vmem),
        scratch_shapes=scratch,
        compiler_params=pltpu.CompilerParams(
            collective_id=0, has_side_effects=True, vmem_limit_bytes=60 * MIB
        ),
        name="whole_step",
    )(entity, relation, heads, tails, negs, relation_ids)


def local(
    entity_emb,
    entity_state,
    relation_emb,
    relation_state,
    head_rows,
    tail_rows,
    relation_ids,
    negative_rows,
):
    entity = entity_emb.T
    relation_grad, entity_grad = whole_step(
        entity, relation_emb, head_rows, tail_rows, negative_rows, relation_ids
    )
    entity_grad = entity_grad.astype(F32)
    new_entity_state = entity_state + jnp.mean(entity_grad * entity_grad, axis=0)
    new_entity = entity - LEARN_RATE * entity_grad / jnp.sqrt(new_entity_state)
    relation_grad = relation_grad[:OWN_REL, :D]
    new_relation_state = relation_state + jnp.mean(relation_grad * relation_grad, axis=-1)
    new_relation_emb = relation_emb - LEARN_RATE * relation_grad / jnp.sqrt(new_relation_state)[:, None]
    return (new_entity.T, new_entity_state, new_relation_emb, new_relation_state)


def solution(mesh):
    placed = (
        P("dom", None),
        P("dom"),
        P(("dom", "edge"), None),
        P(("dom", "edge")),
        P(None, ("dom", "edge")),
        P(None, ("dom", "edge")),
        P(None, ("dom", "edge")),
        P(None, ("dom", "edge"), None),
    )
    return jax.shard_map(
        local,
        mesh=mesh,
        in_specs=placed,
        out_specs=(P("dom", None), P("dom"), P(("dom", "edge"), None), P(("dom", "edge"))),
        check_vma=False,
    )
```

time: 1040 us -> 136 us (0.13); the launches traced: 1020 us -> 136 us
  waiting for transfers between devices: 776 us -> 0 us
  Pallas kernels: 0 us -> 127 us
  local copies, waits for them, and re-layouts: 110 us -> 0.02 us
  other arithmetic: 80.3 us -> 7.65 us
  starting transfers between devices: 28.5 us -> 0 us
  between operations: 15.5 us -> 0.67 us
    all_gather x1 -> x0, waiting for transfers between devices: 384 us -> none  [local(): lax.all_gather(relation_emb.astype(jnp.bfloat16), ('dom', 'edge'), axis=0...]
    ppermute x4 -> x0, waiting for transfers between devices: 304 us -> none  [shifted(): return lax.ppermute(value, axis, pairs)]
    pallas_call x0 -> x1, Pallas kernels: none -> 127 us  [whole_step(): pl.pallas_call(step_kernel, out_shape=(jax.ShapeDtypeStruct((SLOT, 512),...]
    psum x1 -> x0, waiting for transfers between devices: 88.1 us -> none  [local(): entity_grad = lax.psum(local_total, 'edge')]
    scatter-add x5 -> x0, other arithmetic: 38.2 us -> none  [the longest x1 13.6 us: local(): jnp.zeros((rel_total, features), jnp.float32).at[all_ids].add(all_grads)]
    reshape x2 -> x0, local copies, waits for them, and re-layouts: 31.3 us -> none  [local(): arranged = grad_table.reshape(dom_count, edge_count * own_count, features)]
    gather x14 -> x0, local copies, waits for them, and re-layouts: 30.4 us -> none  [the longest x4 13.9 us: bucket_terms(): rel_vec = relation_table[relation_index].astype(jnp.float32)]
    unnamed x62 -> x10, local copies, waits for them, and re-layouts: 23.8 us -> 0.02 us
  transfers between devices with their start and end apart: 8 -> 0, of which waited for: 5 -> 0; matrix products, arithmetic and copies ran while one was open for 10% -> 0% of each run, Pallas kernels for 0% -> 0%
where the time goes in v2:
time: 136 us
  Pallas kernels  127 us (93%)
  other arithmetic  7.65 us (6%)
    pallas_call x1, Pallas kernels, whole_step(): pl.pallas_call(step_kernel, out_shape=(jax.ShapeDtypeStruct((SLOT, 512),...  127 us
    transpose x1, other arithmetic, local(): return (new_entity.T, new_entity_state, new_relation_emb, new_relation_st...  3.93 us

profile of v2, /device:TPU:1, one launch (start us, length us, event | category | flops | bytes accessed | tf_op | source)
XLA Modules:
  0.0 135.6 jit_solution(3165092561497482157)
XLA Ops:
  0.6 0.0 copy-start
  0.6 0.0 copy-start.3
  0.7 127.3 %whole_step.1 = (f32[32,512]{1,0:T(8,128)}, bf16[400,2048]{1,0:T(8,128)(2,1)}) custom-call(f32[400,2048]{1,0:T(8,128)} %bitcast.4, f32[29,400]{1,0:T(8,128)} %relation.1, s32[2,512]{1,0:T(2,128)} %heads.1, s32[2,512]{1,0:T(2,128)} %tails.1, s32[2,1,256]{2,1,0:T(1,128)} %negs.1, s32[2,512]{1,0:T(2,128)} %relation_ids.1), custom_call_target="tpu_custom_call" | custom-call | tf_op jit(solution)/shard_map/whole_step/pallas_call | solution.py:516
  127.9 1.8 %fusion.3 = f32[2048]{0:T(1024)S(1)} fusion(bf16[400,2048]{1,0:T(8,128)(2,1)} %get-tuple-element.6), kind=kLoop, calls=%fused_computation.5 | loop fusion | flops 2455552 | bytes 1646592 | tf_op jit(solution)/shard_map/reduce_sum | solution.py:547
  129.7 0.0 copy-done.3
  129.7 0.6 fusion.5
  130.3 0.0 copy-done
  130.3 0.0 copy-start.2
  130.3 0.0 copy-start.4
  130.3 0.0 copy-start.1
  130.3 3.9 %fusion.2 = f32[2048,400]{0,1:T(8,128)} fusion(bf16[400,2048]{1,0:T(8,128)(2,1)} %get-tuple-element.6, f32[2048]{0:T(1024)S(1)} %get-tuple-element.10, f32[2048,400]{0,1:T(8,128)S(1)} %copy-done), kind=kLoop, calls=%fused_computation.4 | loop fusion | flops 3276800 | bytes 8200192 | tf_op jit(solution)/shard_map/transpose | solution.py:552
  134.3 0.0 copy-done.2
  134.3 0.1 multiply_reduce_fusion
  134.4 0.0 copy-done.4
  134.4 0.5 fusion.4
  134.9 0.0 copy-done.1
  134.9 0.7 divide_subtract_fusion
Async XLA Ops:
  0.6 129.7 %copy-start = (f32[2048,400]{0,1:T(8,128)S(1)}, f32[2048,400]{0,1:T(8,128)}, u32[]{:S(2)}) copy-start(f32[2048,400]{0,1:T(8,128)} %param.8) | copy-start | bytes 9830404
  0.6 129.1 %copy-start.3 = (f32[2048]{0:T(1024)S(1)}, f32[2048]{0:T(1024)}, u32[]{:S(2)}) copy-start(f32[2048]{0:T(1024)} %param.9) | copy-start | bytes 24580
  130.3 3.9 %copy-start.2 = (f32[32,512]{1,0:T(8,128)S(1)}, f32[32,512]{1,0:T(8,128)}, u32[]{:S(2)}) copy-start(f32[32,512]{1,0:T(8,128)} %get-tuple-element.7) | copy-start | bytes 196612
  130.3 4.1 %copy-start.4 = (f32[29]{0:T(128)S(1)}, f32[29]{0:T(128)}, u32[]{:S(2)}) copy-start(f32[29]{0:T(128)} %param.11) | copy-start | bytes 352
  130.3 4.6 %copy-start.1 = (f32[29,400]{1,0:T(8,128)S(1)}, f32[29,400]{1,0:T(8,128)}, u32[]{:S(2)}) copy-start(f32[29,400]{1,0:T(8,128)} %relation.1) | copy-start | bytes 139204

commit v3 on v2

--- a/solution.py
+++ b/solution.py
@@ -31,6 +31,7 @@
         self.y = lax.rem(self.d, 4)
         self.z = lax.rem(self.d // 4, Z)
         self.xl = self.d // 32
+        self.even = jnp.logical_and(self.y > 0, self.y < 3)
         self.xh = self.e // 2
         self.c = lax.rem(self.e, 2)
         x = self.xh * 2 + self.xl
@@ -53,8 +54,20 @@
     def block(self, xl, offset, half):
         return (xl * Z + lax.rem(self.z + offset + Z, Z)) * 2 + half
 
+    def ring_step(self, j):
+        return (jnp.where(self.even, 0x32211000, 0x43121000) >> (4 * jnp.minimum(j, 7))) & 15
+
+    def ring_way(self, j):
+        return (jnp.where(self.even, 0x54, jnp.where(self.y == 0, 0x24, 0xDA)) >> j) & 1
+
+    def ring_sent(self, way, step, part):
+        most = jnp.where(self.even, jnp.where(part == way, 4, 3), jnp.where(way == self.y // 3, 5, 2))
+        return step < most
+
     def incoming(self, j, xl, half):
-        return self.block(xl, jnp.where(j % 2 == 1, -((j + 1) // 2), j // 2), half)
+        away = self.ring_step(j) + 1
+        away = jnp.where(self.ring_way(j) == 1, away, -away)
+        return self.block(xl, jnp.where(j == 0, 0, away), half)
 
     def outgoing(self, j, xl, half):
         away = 4 - (j + 1) // 2
@@ -71,7 +84,7 @@
         )
     for peer in (at.x_up, at.x_down, at.z_up, at.z_down, at.next, at.prev):
         pl.semaphore_signal(barrier, inc=1, device_id=peer, device_id_type=MESH)
-    pl.semaphore_wait(barrier, 21)
+    return barrier
 
 
 def send(src, dst, send_sem, recv_sem, peer):
@@ -105,6 +118,7 @@
 BLOCK = (D, 256)
 DMA = pltpu.SemaphoreType.DMA
 BUFFERS = (
+    ("entity", (D, ROWS), F32),
     ("pad", (SLOT, 512), F32),
     ("shard", (SLOT, 512), BF),
     ("own", (D, ROWS), BF),
@@ -134,13 +148,13 @@
     ("ent_sum", (4,) + BLOCK, BF),
     ("ent_far", (4,) + BLOCK, BF),
     ("ent_end", (8,) + BLOCK, BF),
-    ("fin", (256, 512), F32),
-    ("parts", (8, SLOT, 512), F32),
+    ("fin", (256, 512), BF),
+    ("parts", (8, SLOT, 512), BF),
 )
 SEMAPHORES = (
-    ("a", (8,)), ("i", (2,)), ("p", (2, 3)), ("z", (2, 4)), ("x", (2, 8)), ("s", (16,)),
-    ("n", (2, 3)), ("t", (16,)), ("w", (2, 8)), ("v", (2, 4)),
-    ("es", (4,)), ("ef", (4,)), ("ee", (4,)), ("c", (8,)),
+    ("a", (8,)), ("i", (2,)), ("p", (2, 3)), ("z", (2, 2, 5)), ("x", (2, 8)), ("s", (16,)),
+    ("n", (2, 3)), ("t", (16,)), ("w", (2, 8)), ("v", (2, 2, 4)),
+    ("es", (4,)), ("ef", (4,)), ("ee", (4,)), ("c", (8,)), ("o", (9,)),
 )
 
 
@@ -148,7 +162,9 @@
     pass
 
 
-def step_kernel(entity, relation, heads, tails, negs, relation_ids, rel_out, ent_out, *scratch):
+def step_kernel(
+    entity_in, entity_state, relation, heads, tails, negs, relation_ids, rel_out, ent_out, state_out, *scratch
+):
     m = Held()
     names = [name for name, _, _ in BUFFERS]
     for name, _ in SEMAPHORES:
@@ -158,8 +174,10 @@
     at = Place()
     top, low = pl.ds(0, CUT), pl.ds(CUT, D - CUT)
     halves = (top, low)
-
-    m.own[...] = entity[...].astype(BF)
+    barrier = greet(at)
+    load = pltpu.make_async_copy(entity_in, m.entity, m.o_recv.at[8])
+    load.start()
+
     m.pad[...] = jnp.zeros_like(m.pad)
     m.pad[:OWN_REL, :D] = relation[...]
     m.shard[...] = m.pad[...].astype(BF)
@@ -168,7 +186,7 @@
         m.ids_out[b, :, EDGES:] = jnp.broadcast_to(negs[b], (8, NEG))
     ids = relation_ids[...]
     m.rels[...] = ids + (SLOT - OWN_REL) * ((ids * 36158) >> 20)
-    greet(at)
+    pl.semaphore_wait(barrier, 21)
 
     slot = lax.rem(at.y, 2) * 4 + at.e
     here = at.c == at.y // 2
@@ -188,31 +206,32 @@
             send(m.shard, mine, m.a_send.at[k], m.a_recv.at[slot], peer)
     for b, peer in enumerate((at.next, at.prev)):
         send(m.ids_out.at[b], m.ids.at[b], m.i_send.at[b], m.i_recv.at[b], peer)
+    load.wait()
+    m.own[...] = m.entity[...].astype(BF)
 
     for k in range(8):
         settle(m.gath.at[pl.ds(k * SLOT, SLOT), :], m.a_recv.at[k])
     m.table[at.block(at.xl, 0, at.c)] = m.gath[...].astype(F32).T[:D].astype(BF)
 
-    def along_z(j, way, step):
-        ref = m.table.at[at.incoming(j, at.xl, at.c)]
-        send(ref, ref, m.z_send.at[way, step], m.z_recv.at[way, step], at.along_z(way))
-
-    def half_along_z(j, way):
-        ref = m.table.at[at.incoming(j, at.xl, at.c), halves[way], :]
-        send(ref, ref, m.z_send.at[way, 3], m.z_recv.at[way, 3], at.along_z(way))
-
-    def along_x(j):
-        for way, peer in ((0, at.x_up), (1, at.x_down)):
-            ref = m.table.at[at.incoming(j, at.xl, at.c), halves[way], :]
-            send(ref, ref, m.x_send.at[way, j], m.x_recv.at[way, j], peer)
+    def ring_block(j, part):
+        return m.table.at[at.incoming(j, at.xl, at.c), halves[part], :]
+
+    def along_z(j, way, step, part):
+        ref = ring_block(j, part)
+        send(ref, ref, m.z_send.at[part, way, step], m.z_recv.at[part, way, step], at.along_z(way))
+
+    def along_x(j, part):
+        ref = ring_block(j, part)
+        send(ref, ref, m.x_send.at[part, j], m.x_recv.at[part, j], (at.x_up, at.x_down)[part])
 
     def to_sibling(j, xl, q):
         ref = m.table.at[at.incoming(j, xl, at.c)]
         send(ref, ref, m.s_send.at[q], m.s_recv.at[q], at.sibling)
 
-    along_z(0, 0, 0)
-    along_z(0, 1, 0)
-    along_x(0)
+    for part in range(2):
+        along_z(0, 0, 0, part)
+        along_z(0, 1, 0, part)
+        along_x(0, part)
     to_sibling(0, at.xl, 0)
 
     for b in range(2):
@@ -234,63 +253,61 @@
             m.own[...], onehot(heads[pl.ds(t // 2, 1), lanes(t % 2)], 0, ROWS)
         )
 
-    @pl.loop(1, 10)
+    def absorb(k, xl, q):
+        settle(m.table.at[at.incoming(k, xl, 1 - at.c)], m.s_recv.at[q])
+        n, other = at.incoming(k, xl, 0), at.incoming(k, xl, 1)
+        for b in range(2):
+            m.rel_vec[:, b * EDGES:(b + 1) * EDGES] += dot(
+                m.table[n], onehot(m.rels[b:b + 1, :], n * 256, 256)
+            ) + dot(m.table[other], onehot(m.rels[b:b + 1, :], other * 256, 256))
+
+    @pl.loop(1, 12)
     def _(j):
-        way = (j + 1) % 2
-
-        @pl.when(j <= 6)
-        def _():
-            settle(m.table.at[at.incoming(j, at.xl, at.c)], m.z_recv.at[way, (j - 1) // 2])
-
-        @pl.when(j == 7)
-        def _():
-            for side in range(2):
-                settle(m.table.at[at.incoming(j, at.xl, at.c), halves[side], :], m.z_recv.at[side, 3])
+        way, step = at.ring_way(j), at.ring_step(j)
+        split = jnp.logical_and(at.even, j == 7)
+        for part in range(2):
+            @pl.when(jnp.logical_and(j <= 7, jnp.logical_not(split)))
+            def _():
+                settle(ring_block(j, part), m.z_recv.at[part, way, step])
+
+            @pl.when(split)
+            def _():
+                settle(ring_block(j, part), m.z_recv.at[part, part, 3])
+
+            @pl.when(jnp.logical_and(j <= 6, at.ring_sent(way, step + 1, part)))
+            def _():
+                along_z(j, way, step + 1, part)
+
+            @pl.when(j <= 7)
+            def _():
+                along_x(j, part)
+
+        @pl.when(j <= 7)
+        def _():
+            to_sibling(j, at.xl, j)
+
+        @pl.when(jnp.logical_and(j >= 2, j <= 9))
+        def _():
+            for part in range(2):
+                settle(
+                    m.table.at[at.incoming(j - 2, 1 - at.xl, at.c), halves[part], :],
+                    m.x_recv.at[part, j - 2],
+                )
+            to_sibling(j - 2, 1 - at.xl, 6 + j)
 
         @pl.when(j <= 4)
         def _():
-            along_z(j, way, (j + 1) // 2)
-
-        @pl.when(j == 5)
-        def _():
-            half_along_z(j, 0)
-
-        @pl.when(j == 6)
-        def _():
-            half_along_z(j, 1)
-
-        @pl.when(j <= 7)
-        def _():
-            along_x(j)
-            to_sibling(j, at.xl, j)
-
-        @pl.when(j <= 8)
-        def _():
-            for side in range(2):
-                settle(
-                    m.table.at[at.incoming(j - 1, 1 - at.xl, at.c), halves[side], :],
-                    m.x_recv.at[side, j - 1],
-                )
-            to_sibling(j - 1, 1 - at.xl, 7 + j)
-
-        @pl.when(j <= 4)
-        def _():
             head_rows(j - 1)
 
-        @pl.when(j >= 2)
-        def _():
-            k = j - 2
-            for xl, q in ((at.xl, k), (1 - at.xl, 8 + k)):
-                settle(m.table.at[at.incoming(k, xl, 1 - at.c)], m.s_recv.at[q])
-            for b in range(2):
-                total = None
-                for xl in range(2):
-                    for half in range(2):
-                        n = at.incoming(k, xl, half)
-                        term = dot(m.table[n], onehot(m.rels[b:b + 1, :], n * 256, 256))
-                        total = term if total is None else total + term
-                m.rel_vec[:, b * EDGES:(b + 1) * EDGES] += total
-
+        @pl.when(jnp.logical_and(j >= 2, j <= 9))
+        def _():
+            absorb(j - 2, at.xl, j - 2)
+
+        @pl.when(j >= 4)
+        def _():
+            absorb(j - 4, 1 - at.xl, 4 + j)
+
+    kept = []
     for b in range(2):
         for n in range(3):
             settle(m.picked.at[b, n], m.p_recv.at[b, n])
@@ -300,10 +317,9 @@
         q = jnp.concatenate([h_re * r_re - h_im * r_im, h_re * r_im + h_im * r_re], axis=0)
         q_low = q.astype(BF)
         tail = jnp.concatenate([m.picked[b, 0], m.picked[b, 1]], axis=1).astype(F32)
-        cand = m.picked[b, 2]
         positive = jnp.sum(q * tail, axis=0, keepdims=True)
         slope = -jax.nn.sigmoid(-positive)
-        scores = dot(cand, q_low, ((0,), (0,)))
+        scores = dot(m.picked[b, 2], q_low, ((0,), (0,)))
         neg_slope = jax.nn.sigmoid(scores).astype(BF)
         tail_grad = (slope * q).astype(BF)
         m.pick_grad[b, 0] = tail_grad[:, :256]
@@ -314,7 +330,15 @@
                 m.pick_grad.at[b, n], m.pick_in.at[b, n], m.n_send.at[b, n], m.n_recv.at[b, n],
                 (at.next, at.prev)[b],
             )
-        u = slope * tail + dot(cand, neg_slope)
+        kept.append((slope, neg_slope))
+
+    for b in range(2):
+        span = slice(b * EDGES, (b + 1) * EDGES)
+        h_re, h_im = m.head_vec[:HALF, span], m.head_vec[HALF:, span]
+        r_re, r_im = m.rel_vec[:HALF, span], m.rel_vec[HALF:, span]
+        slope, neg_slope = kept[b]
+        tail = jnp.concatenate([m.picked[b, 0], m.picked[b, 1]], axis=1).astype(F32)
+        u = slope * tail + dot(m.picked[b, 2], neg_slope)
         u_re, u_im = u[:HALF], u[HALF:]
         m.rel_grad[:, span] = jnp.concatenate(
             [u_re * h_re + u_im * h_im, u_im * h_re - u_re * h_im], axis=0
@@ -386,34 +410,30 @@
         m.acc[...] = total + m.sib[8 + j].astype(F32) + m.xbuf[j].astype(F32)
         way, step = (j + 1) % 2, (j + 1) // 2
 
-        for side in range(2):
-            @pl.when(j == side + 1)
-            def _():
-                settle(m.zbuf.at[side, 0, halves[side], :], m.v_recv.at[side, 0])
-                rows = (slice(0, CUT), slice(CUT, D))[side]
-                m.acc[rows, :] += m.zbuf[side, 0, rows, :].astype(F32)
-
-        @pl.when(jnp.logical_and(j >= 3, j <= 6))
-        def _():
-            settle(m.zbuf.at[way, step - 1], m.v_recv.at[way, step - 1])
-            m.acc[...] += m.zbuf[way, step - 1].astype(F32)
-
-        @pl.when(j == 0)
-        def _():
-            m.zs[0] = m.acc[...].astype(BF)
-            for side in range(2):
+        for part in range(2):
+            rows = (slice(0, CUT), slice(CUT, D))[part]
+
+            def add(side, last):
+                settle(m.zbuf.at[side, last, halves[part], :], m.v_recv.at[part, side, last])
+                m.acc[rows, :] += m.zbuf[side, last, rows, :].astype(F32)
+
+            @pl.when(jnp.logical_or(j == part + 1, jnp.logical_and(j >= 3, j <= 6)))
+            def _():
+                add(way, step - 1)
+
+            @pl.when(j == 7)
+            def _():
+                add(0, 3)
+                add(1, 3)
+
+            @pl.when(j <= 6)
+            def _():
+                m.zs[j, rows, :] = m.acc[rows, :].astype(BF)
+                side = jnp.where(j == 0, part, way)
                 send(
-                    m.zs.at[0, halves[side], :], m.zbuf.at[side, 0, halves[side], :],
-                    m.v_send.at[side, 0], m.v_recv.at[side, 0], at.along_z(side),
+                    m.zs.at[j, halves[part], :], m.zbuf.at[side, step, halves[part], :],
+                    m.v_send.at[part, side, step], m.v_recv.at[part, side, step], at.along_z(side),
                 )
-
-        @pl.when(jnp.logical_and(j >= 1, j <= 6))
-        def _():
-            m.zs[j] = m.acc[...].astype(BF)
-            send(
-                m.zs.at[j], m.zbuf.at[way, step], m.v_send.at[way, step], m.v_recv.at[way, step],
-                at.along_z(way),
-            )
 
         @pl.when(j < 4)
         def _():
@@ -426,22 +446,17 @@
                 for n in range(3):
                     settle(m.pick_in.at[b, n], m.n_recv.at[b, n])
 
-        @pl.when(jnp.logical_or(j == 4, j == 5))
-        def _():
-            @pl.loop(0, 2)
+            @pl.loop(0, 5)
             def _(i):
-                entity_swap(2 * (j - 4) + i)
-
-        @pl.when(j >= 6)
-        def _():
-            @pl.loop(0, 2)
-            def _(i):
-                entity_far(2 * (j - 6) + i)
-
-    for side in range(2):
-        settle(m.zbuf.at[side, 3], m.v_recv.at[side, 3])
-    total = m.acc[...] + m.zbuf[0, 3].astype(F32) + m.zbuf[1, 3].astype(F32)
-    m.fin[...] = jnp.concatenate([total, jnp.zeros((512 - D, 256), F32)], axis=0).T
+                @pl.when(i < 4)
+                def _():
+                    entity_swap(i)
+
+                @pl.when(i > 0)
+                def _():
+                    entity_far(i - 1)
+
+    m.fin[...] = jnp.concatenate([m.acc[...], jnp.zeros((512 - D, 256), F32)], axis=0).T.astype(BF)
     source = at.y * 2 + at.xh
     for k in range(8):
         y, e = 2 * at.c + k // 4, k % 4
@@ -465,11 +480,25 @@
 
     for k in range(8):
         settle(m.parts.at[k], m.c_recv.at[k])
-    rel_out[...] = jnp.sum(m.parts[...], axis=0)
-    for k in range(4):
+    rel_out[...] = jnp.sum(m.parts[...].astype(F32), axis=0)
+    def adagrad(n):
+        grad = m.ent_end[n].astype(F32)
+        history = entity_state[:, lanes(n)] + jnp.sum(grad * grad, axis=0, keepdims=True) * (1.0 / D)
+        state_out[:, lanes(n)] = history
+        m.entity[:, lanes(n)] -= grad * (LEARN_RATE / jnp.sqrt(history))
+        pltpu.make_async_copy(m.entity.at[:, lanes(n)], ent_out.at[:, lanes(n)], m.o_recv.at[n]).start()
+
+    @pl.loop(0, 4)
+    def _(k):
+        adagrad(at.c * 4 + k)
+
+    @pl.loop(0, 4)
+    def _(k):
         settle(m.ent_end.at[(1 - at.c) * 4 + k], m.ee_recv.at[k])
+        adagrad((1 - at.c) * 4 + k)
+
     for n in range(8):
-        ent_out[:, n * 256:(n + 1) * 256] = m.ent_end[n]
+        pltpu.make_async_copy(m.entity.at[:, lanes(n)], ent_out.at[:, lanes(n)], m.o_recv.at[n]).wait()
 
     @pl.when(jnp.logical_not(here))
     def _():
@@ -491,11 +520,15 @@
             settle(one, m.p_send.at[b, n])
             settle(one, m.n_send.at[b, n])
         half = m.stage.at[0, halves[b], :]
-        for step in range(3):
-            settle(one, m.z_send.at[b, step])
-            settle(one, m.v_send.at[b, step + 1])
-        settle(half, m.z_send.at[b, 3])
-        settle(half, m.v_send.at[b, 0])
+        for way in range(2):
+            for step in range(5):
+                @pl.when(at.ring_sent(way, step, b))
+                def _():
+                    settle(half, m.z_send.at[b, way, step])
+
+            for step in range(3):
+                settle(half, m.v_send.at[b, way, step + 1])
+        settle(half, m.v_send.at[b, b, 0])
         for j in range(8):
             settle(half, m.x_send.at[b, j])
             settle(half, m.w_send.at[b, j])
@@ -508,8 +541,9 @@
         settle(one, m.ee_send.at[k])
 
 
-def whole_step(entity, relation, heads, tails, negs, relation_ids):
+def whole_step(entity, entity_state, relation, heads, tails, negs, relation_ids):
     vmem = pl.BlockSpec(memory_space=pltpu.VMEM)
+    anywhere = pl.BlockSpec(memory_space=pl.ANY)
     scratch = [pltpu.VMEM(shape, kind) for _, shape, kind in BUFFERS]
     for _, shape in SEMAPHORES:
         scratch += [DMA(shape), DMA(shape)]
@@ -517,16 +551,17 @@
         step_kernel,
         out_shape=(
             jax.ShapeDtypeStruct((SLOT, 512), F32),
-            jax.ShapeDtypeStruct((D, ROWS), BF),
+            jax.ShapeDtypeStruct((D, ROWS), F32),
+            jax.ShapeDtypeStruct((1, ROWS), F32),
         ),
-        in_specs=[vmem] * 6,
-        out_specs=(vmem, vmem),
+        in_specs=[anywhere] + [vmem] * 6,
+        out_specs=(vmem, anywhere, vmem),
         scratch_shapes=scratch,
         compiler_params=pltpu.CompilerParams(
             collective_id=0, has_side_effects=True, vmem_limit_bytes=60 * MIB
         ),
         name="whole_step",
-    )(entity, relation, heads, tails, negs, relation_ids)
+    )(entity, entity_state, relation, heads, tails, negs, relation_ids)
 
 
 def local(
@@ -539,17 +574,13 @@
     relation_ids,
     negative_rows,
 ):
-    entity = entity_emb.T
-    relation_grad, entity_grad = whole_step(
-        entity, relation_emb, head_rows, tail_rows, negative_rows, relation_ids
+    relation_grad, new_entity, new_entity_state = whole_step(
+        entity_emb.T, entity_state[None], relation_emb, head_rows, tail_rows, negative_rows, relation_ids
     )
-    entity_grad = entity_grad.astype(F32)
-    new_entity_state = entity_state + jnp.mean(entity_grad * entity_grad, axis=0)
-    new_entity = entity - LEARN_RATE * entity_grad / jnp.sqrt(new_entity_state)
     relation_grad = relation_grad[:OWN_REL, :D]
     new_relation_state = relation_state + jnp.mean(relation_grad * relation_grad, axis=-1)
     new_relation_emb = relation_emb - LEARN_RATE * relation_grad / jnp.sqrt(new_relation_state)[:, None]
-    return (new_entity.T, new_entity_state, new_relation_emb, new_relation_state)
+    return (new_entity.T, new_entity_state[0], new_relation_emb, new_relation_state)
 
 
 def solution(mesh):

time: 136 us -> 128 us (0.941); the launches traced: 136 us -> 126 us
  Pallas kernels: 127 us -> 118 us
  other arithmetic: 7.65 us -> 3.02 us
  local copies, waits for them, and re-layouts: 0.02 us -> 4.63 us
    pallas_call x1, Pallas kernels: 127 us -> 118 us  [whole_step(): pl.pallas_call(step_kernel, out_shape=(jax.ShapeDtypeStruct((SLOT, 512),...]
    unnamed x10 -> x8, local copies, waits for them, and re-layouts: 0.02 us -> 4.63 us
    transpose x1 -> x0, other arithmetic: 3.93 us -> none  [local(): return (new_entity.T, new_entity_state, new_relation_emb, new_relation_st...]
    reduce_sum x1 -> x0, other arithmetic: 1.78 us -> none  [local(): jnp.mean(entity_grad * entity_grad, axis=0)]
where the time goes in v3:
time: 128 us; the launch traced here: 126 us
  Pallas kernels  118 us (92%)
  local copies, waits for them, and re-layouts  4.63 us (4%)
  other arithmetic  3.02 us (2%)
    pallas_call x1, Pallas kernels, whole_step(): pl.pallas_call(step_kernel, out_shape=(jax.ShapeDtypeStruct((SLOT, 512),...  118 us
    unnamed x8, local copies, waits for them, and re-layouts  4.63 us

profile of v3, /device:TPU:1, one launch (start us, length us, event | category | flops | bytes accessed | tf_op | source)
XLA Modules:
  0.0 126.0 jit_solution(11925597985420717098)
XLA Ops:
  0.6 0.0 copy-start
  0.6 0.0 copy-start.2
  0.7 117.6 %whole_step.1 = (f32[32,512]{1,0:T(8,128)}, f32[400,2048]{1,0:T(8,128)}, f32[1,2048]{1,0:T(1,128)}) custom-call(f32[400,2048]{1,0:T(8,128)} %bitcast.5, f32[1,2048]{1,0:T(1,128)} %bitcast.6, f32[29,400]{1,0:T(8,128)} %relation.1, s32[2,512]{1,0:T(2,128)} %heads.1, s32[2,512]{1,0:T(2,128)} %tails.1, s32[2,1,256]{2,1,0:T(1,128)} %negs.1, s32[2,512]{1,0:T(2,128)} %relation_ids.1), custom_call_target="tpu_custom_call" | custom-call | tf_op jit(solution)/shard_map/whole_step/pallas_call | solution.py:550
  118.3 1.0 multiply_reduce_fusion
  119.3 0.0 copy-done.2
  119.3 0.5 fusion
  119.8 0.0 copy-done
  119.8 1.5 %divide_subtract_fusion = f32[29,400]{1,0:T(8,128)} fusion(f32[29,400]{1,0:T(8,128)S(1)} %copy-done, f32[32,512]{1,0:T(8,128)} %get-tuple-element.9, f32[29]{0:T(128)S(1)} %get-tuple-element.10), kind=kLoop, calls=%fused_computation | loop fusion | flops 34800 | bytes 139316 | tf_op jit(solution)/shard_map/sub | solution.py:582
  121.3 0.0 copy-start.1
  121.3 4.0 %copy.14 = f32[2048,400]{0,1:T(8,128)} copy(f32[2048,400]{0,1:T(8,128)} %bitcast.4) | data formatting | bytes 6553600
  125.4 0.0 copy-done.1
  125.4 0.6 copy.15
Async XLA Ops:
  0.6 119.1 %copy-start = (f32[29,400]{1,0:T(8,128)S(1)}, f32[29,400]{1,0:T(8,128)}, u32[]{:S(2)}) copy-start(f32[29,400]{1,0:T(8,128)} %relation.1) | copy-start | bytes 139204
  0.6 118.6 %copy-start.2 = (f32[29]{0:T(128)S(1)}, f32[29]{0:T(128)}, u32[]{:S(2)}) copy-start(f32[29]{0:T(128)} %param.11) | copy-start | bytes 352
  121.3 4.0 %copy-start.1 = (f32[1,2048]{1,0:T(1,128)S(1)}, f32[1,2048]{1,0:T(1,128)}, u32[]{:S(2)}) copy-start(f32[1,2048]{1,0:T(1,128)} %get-tuple-element.8) | copy-start | bytes 24580

commit v4 on v3

--- a/solution.py
+++ b/solution.py
@@ -105,6 +105,19 @@
 def onehot(ids, base, rows):
     at = lax.broadcasted_iota(jnp.int32, (rows, ids.shape[1]), 0) + base
     return jnp.where(at == ids, 1.0, 0.0).astype(BF)
+
+
+def columns(ids):
+    return jnp.broadcast_to(ids, (128, ids.shape[1])).T
+
+
+def spread(cols, bases):
+    lane = lax.broadcasted_iota(jnp.int32, cols.shape, 1)
+    tiles = []
+    for base in bases:
+        for k in (0, 128):
+            tiles.append(jnp.where(cols - (base + k) == lane, 1.0, 0.0).astype(BF))
+    return jnp.concatenate(tiles, axis=1)
 
 
 def dot(a, b, over=((1,), (0,))):
@@ -139,6 +152,11 @@
     ("sib", (16,) + BLOCK, BF),
     ("xs", (8,) + BLOCK, BF),
     ("xbuf", (8,) + BLOCK, BF),
+    ("rel_cols", (2 * EDGES, 128), jnp.int32),
+    ("head_cols", (2 * EDGES, 128), jnp.int32),
+    ("pick_cols", (2 * PICKS, 128), jnp.int32),
+    ("beside", (2,) + BLOCK, F32),
+    ("within", (8,) + BLOCK, F32),
     ("acc", BLOCK, F32),
     ("zs", (7,) + BLOCK, BF),
     ("zbuf", (2, 4) + BLOCK, BF),
@@ -208,6 +226,9 @@
         send(m.ids_out.at[b], m.ids.at[b], m.i_send.at[b], m.i_recv.at[b], peer)
     load.wait()
     m.own[...] = m.entity[...].astype(BF)
+    for b in range(2):
+        m.rel_cols[b * EDGES:(b + 1) * EDGES, :] = columns(m.rels[b:b + 1, :])
+        m.head_cols[b * EDGES:(b + 1) * EDGES, :] = columns(heads[b:b + 1, :])
 
     for k in range(8):
         settle(m.gath.at[pl.ds(k * SLOT, SLOT), :], m.a_recv.at[k])
@@ -246,6 +267,8 @@
             (lax.rem(at.d + 63 + 2 * b, 64), at.e),
         )
 
+    for b in range(2):
+        m.pick_cols[b * PICKS:(b + 1) * PICKS, :] = columns(m.ids[b, 0:1, :])
     m.rel_vec[...] = jnp.zeros_like(m.rel_vec)
 
     def head_rows(t):
@@ -347,67 +370,54 @@
             [u_re * r_re + u_im * r_im, u_im * r_re - u_re * r_im], axis=0
         ).astype(BF)
 
-    def rel_block(n):
-        return dot(
-            m.rel_grad[:, :EDGES], onehot(m.rels[0:1, :], n * 256, 256), ACROSS
-        ) + dot(m.rel_grad[:, EDGES:], onehot(m.rels[1:2, :], n * 256, 256), ACROSS)
-
-    def swap(j, xl, q):
-        m.stage[q] = rel_block(at.outgoing(j, xl, 1 - at.c)).astype(BF)
+    def rel_pair(j, xl, q):
+        mine, other = at.outgoing(j, xl, at.c), at.outgoing(j, xl, 1 - at.c)
+        pair = dot(m.rel_grad[...], spread(m.rel_cols[...], (mine * 256, other * 256)))
+        m.stage[q] = pair[:, 256:].astype(BF)
         send(m.stage.at[q], m.sib.at[q], m.t_send.at[q], m.t_recv.at[q], at.sibling)
-
-    @pl.loop(0, 9)
-    def _(j):
-        @pl.when(j < 8)
-        def _():
-            swap(j, 1 - at.xl, j)
-
-        @pl.when(j > 0)
-        def _():
-            k = j - 1
-            total = rel_block(at.outgoing(k, 1 - at.xl, at.c))
-            settle(m.sib.at[k], m.t_recv.at[k])
-            m.xs[k] = (total + m.sib[k].astype(F32)).astype(BF)
-            for side, peer in ((0, at.x_up), (1, at.x_down)):
-                send(
-                    m.xs.at[k, halves[side], :], m.xbuf.at[k, halves[side], :],
-                    m.w_send.at[side, k], m.w_recv.at[side, k], peer,
-                )
-
-    @pl.loop(0, 8)
-    def _(j):
-        swap(j, at.xl, 8 + j)
-
-    def head_part(n):
-        m.head_sum[n] = dot(
-            m.head_grad[:, :EDGES], onehot(heads[0:1, :], n * 256, 256), ACROSS
-        ) + dot(m.head_grad[:, EDGES:], onehot(heads[1:2, :], n * 256, 256), ACROSS)
-
-    def entity_block(n):
-        total = m.head_sum[n]
+        return pair[:, :256]
+
+    def to_x(k):
+        settle(m.sib.at[k], m.t_recv.at[k])
+        m.xs[k] = (m.beside[k % 2] + m.sib[k].astype(F32)).astype(BF)
+        for side, peer in ((0, at.x_up), (1, at.x_down)):
+            send(
+                m.xs.at[k, halves[side], :], m.xbuf.at[k, halves[side], :],
+                m.w_send.at[side, k], m.w_recv.at[side, k], peer,
+            )
+
+    def head_pair(k):
+        pair = dot(m.head_grad[...], spread(m.head_cols[...], (k * 512, k * 512 + 256)))
+        m.head_sum[2 * k] = pair[:, :256]
+        m.head_sum[2 * k + 1] = pair[:, 256:]
+
+    def entity_pair(k):
+        total = None
         for b in range(2):
             for i in range(3):
-                ids = m.ids[b, 0:1, i * 256:(i + 1) * 256]
-                total = total + dot(m.pick_in[b, i], onehot(ids, n * 256, 256), ACROSS)
-        return total
+                start = b * PICKS + i * 256
+                term = dot(
+                    m.pick_in[b, i],
+                    spread(m.pick_cols[start:start + 256, :], (k * 512, k * 512 + 256)),
+                )
+                total = term if total is None else total + term
+        m.head_sum[2 * k] += total[:, :256]
+        m.head_sum[2 * k + 1] += total[:, 256:]
 
     def entity_swap(k):
-        m.ent_stage[k] = entity_block((1 - at.c) * 4 + k).astype(BF)
+        m.ent_stage[k] = m.head_sum[(1 - at.c) * 4 + k].astype(BF)
         send(m.ent_stage.at[k], m.ent_sib.at[k], m.es_send.at[k], m.es_recv.at[k], at.sibling)
 
     def entity_far(k):
-        total = entity_block(at.c * 4 + k)
         settle(m.ent_sib.at[k], m.es_recv.at[k])
-        m.ent_sum[k] = (total + m.ent_sib[k].astype(F32)).astype(BF)
+        m.ent_sum[k] = (m.head_sum[at.c * 4 + k] + m.ent_sib[k].astype(F32)).astype(BF)
         send(m.ent_sum.at[k], m.ent_far.at[k], m.ef_send.at[k], m.ef_recv.at[k], at.far)
 
-    @pl.loop(0, 8)
-    def _(j):
-        total = rel_block(at.outgoing(j, at.xl, at.c))
+    def z_step(j):
         settle(m.sib.at[8 + j], m.t_recv.at[8 + j])
         for side in range(2):
             settle(m.xbuf.at[j, halves[side], :], m.w_recv.at[side, j])
-        m.acc[...] = total + m.sib[8 + j].astype(F32) + m.xbuf[j].astype(F32)
+        m.acc[...] = m.within[j] + m.sib[8 + j].astype(F32) + m.xbuf[j].astype(F32)
         way, step = (j + 1) % 2, (j + 1) // 2
 
         for part in range(2):
@@ -435,26 +445,45 @@
                     m.v_send.at[part, side, step], m.v_recv.at[part, side, step], at.along_z(side),
                 )
 
-        @pl.when(j < 4)
-        def _():
-            head_part(2 * j)
-            head_part(2 * j + 1)
-
-        @pl.when(j == 4)
+    @pl.loop(0, 11)
+    def _(j):
+        @pl.when(j < 8)
+        def _():
+            m.beside[j % 2] = rel_pair(j, 1 - at.xl, j)
+
+        @pl.when(jnp.logical_and(j >= 1, j <= 8))
+        def _():
+            to_x(j - 1)
+
+        @pl.when(j < 8)
+        def _():
+            m.within[j] = rel_pair(j, at.xl, 8 + j)
+
+        @pl.when(jnp.logical_and(j >= 4, j <= 7))
+        def _():
+            head_pair(j - 4)
+
+        @pl.when(j >= 3)
+        def _():
+            z_step(j - 3)
+
+        @pl.when(j == 8)
         def _():
             for b in range(2):
                 for n in range(3):
                     settle(m.pick_in.at[b, n], m.n_recv.at[b, n])
 
-            @pl.loop(0, 5)
+            @pl.loop(0, 2)
             def _(i):
-                @pl.when(i < 4)
-                def _():
-                    entity_swap(i)
-
-                @pl.when(i > 0)
-                def _():
-                    entity_far(i - 1)
+                entity_pair((1 - at.c) * 2 + i)
+                entity_swap(2 * i)
+                entity_swap(2 * i + 1)
+
+            @pl.loop(0, 2)
+            def _(i):
+                entity_pair(at.c * 2 + i)
+                entity_far(2 * i)
+                entity_far(2 * i + 1)
 
     m.fin[...] = jnp.concatenate([m.acc[...], jnp.zeros((512 - D, 256), F32)], axis=0).T.astype(BF)
     source = at.y * 2 + at.xh

time: 128 us -> 131 us (1.023); the launches traced: 126 us -> 130 us
  Pallas kernels: 118 us -> 122 us
    pallas_call x1, Pallas kernels: 118 us -> 122 us  [whole_step(): pl.pallas_call(step_kernel, out_shape=(jax.ShapeDtypeStruct((SLOT, 512),...]
where the time goes in v4:
time: 131 us; the launch traced here: 130 us
  Pallas kernels  122 us (93%)
  local copies, waits for them, and re-layouts  4.63 us (4%)
  other arithmetic  3.02 us (2%)
    pallas_call x1, Pallas kernels, whole_step(): pl.pallas_call(step_kernel, out_shape=(jax.ShapeDtypeStruct((SLOT, 512),...  122 us
    unnamed x8, local copies, waits for them, and re-layouts  4.63 us

profile of v4, /device:TPU:1, one launch (start us, length us, event | category | flops | bytes accessed | tf_op | source)
XLA Modules:
  0.0 130.3 jit_solution(2228462001662922007)
XLA Ops:
  0.6 0.0 copy-start
  0.6 0.0 copy-start.2
  0.7 122.0 %whole_step.1 = (f32[32,512]{1,0:T(8,128)}, f32[400,2048]{1,0:T(8,128)}, f32[1,2048]{1,0:T(1,128)}) custom-call(f32[400,2048]{1,0:T(8,128)} %bitcast.5, f32[1,2048]{1,0:T(1,128)} %bitcast.6, f32[29,400]{1,0:T(8,128)} %relation.1, s32[2,512]{1,0:T(2,128)} %heads.1, s32[2,512]{1,0:T(2,128)} %tails.1, s32[2,1,256]{2,1,0:T(1,128)} %negs.1, s32[2,512]{1,0:T(2,128)} %relation_ids.1), custom_call_target="tpu_custom_call" | custom-call | tf_op jit(solution)/shard_map/whole_step/pallas_call | solution.py:579
  122.7 1.0 multiply_reduce_fusion
  123.6 0.0 copy-done.2
  123.6 0.5 fusion
  124.1 0.0 copy-done
  124.1 1.5 %divide_subtract_fusion = f32[29,400]{1,0:T(8,128)} fusion(f32[29,400]{1,0:T(8,128)S(1)} %copy-done, f32[32,512]{1,0:T(8,128)} %get-tuple-element.9, f32[29]{0:T(128)S(1)} %get-tuple-element.10), kind=kLoop, calls=%fused_computation | loop fusion | flops 34800 | bytes 139316 | tf_op jit(solution)/shard_map/sub | solution.py:611
  125.7 0.0 copy-start.1
  125.7 4.0 %copy.14 = f32[2048,400]{0,1:T(8,128)} copy(f32[2048,400]{0,1:T(8,128)} %bitcast.4) | data formatting | bytes 6553600
  129.7 0.0 copy-done.1
  129.7 0.6 copy.15
Async XLA Ops:
  0.6 123.5 %copy-start = (f32[29,400]{1,0:T(8,128)S(1)}, f32[29,400]{1,0:T(8,128)}, u32[]{:S(2)}) copy-start(f32[29,400]{1,0:T(8,128)} %relation.1) | copy-start | bytes 139204
  0.6 123.0 %copy-start.2 = (f32[29]{0:T(128)S(1)}, f32[29]{0:T(128)}, u32[]{:S(2)}) copy-start(f32[29]{0:T(128)} %param.11) | copy-start | bytes 352
  125.7 4.0 %copy-start.1 = (f32[1,2048]{1,0:T(1,128)S(1)}, f32[1,2048]{1,0:T(1,128)}, u32[]{:S(2)}) copy-start(f32[1,2048]{1,0:T(1,128)} %get-tuple-element.8) | copy-start | bytes 24580

commit v5 on v4

--- a/solution.py
+++ b/solution.py
@@ -445,29 +445,29 @@
                     m.v_send.at[part, side, step], m.v_recv.at[part, side, step], at.along_z(side),
                 )
 
-    @pl.loop(0, 11)
+    @pl.loop(0, 9)
     def _(j):
         @pl.when(j < 8)
         def _():
             m.beside[j % 2] = rel_pair(j, 1 - at.xl, j)
 
-        @pl.when(jnp.logical_and(j >= 1, j <= 8))
+        @pl.when(j >= 1)
         def _():
             to_x(j - 1)
 
-        @pl.when(j < 8)
-        def _():
-            m.within[j] = rel_pair(j, at.xl, 8 + j)
-
-        @pl.when(jnp.logical_and(j >= 4, j <= 7))
-        def _():
-            head_pair(j - 4)
-
-        @pl.when(j >= 3)
-        def _():
-            z_step(j - 3)
-
-        @pl.when(j == 8)
+    @pl.loop(0, 8)
+    def _(j):
+        m.within[j] = rel_pair(j, at.xl, 8 + j)
+
+    @pl.loop(0, 8)
+    def _(j):
+        z_step(j)
+
+        @pl.when(j < 4)
+        def _():
+            head_pair(j)
+
+        @pl.when(j == 4)
         def _():
             for b in range(2):
                 for n in range(3):

time: 131 us -> 128 us (0.977)
  Pallas kernels: 122 us -> 118 us
    pallas_call x1, Pallas kernels: 122 us -> 118 us  [whole_step(): pl.pallas_call(step_kernel, out_shape=(jax.ShapeDtypeStruct((SLOT, 512),...]
where the time goes in v5:
time: 128 us; the launch traced here: 126 us
  Pallas kernels  118 us (92%)
  local copies, waits for them, and re-layouts  4.63 us (4%)
  other arithmetic  3.02 us (2%)
    pallas_call x1, Pallas kernels, whole_step(): pl.pallas_call(step_kernel, out_shape=(jax.ShapeDtypeStruct((SLOT, 512),...  118 us
    unnamed x8, local copies, waits for them, and re-layouts  4.63 us

profile of v5, /device:TPU:1, one launch (start us, length us, event | category | flops | bytes accessed | tf_op | source)
XLA Modules:
  0.0 126.5 jit_solution(7804589318132839422)
XLA Ops:
  0.6 0.0 copy-start
  0.6 0.0 copy-start.2
  0.7 118.2 %whole_step.1 = (f32[32,512]{1,0:T(8,128)}, f32[400,2048]{1,0:T(8,128)}, f32[1,2048]{1,0:T(1,128)}) custom-call(f32[400,2048]{1,0:T(8,128)} %bitcast.5, f32[1,2048]{1,0:T(1,128)} %bitcast.6, f32[29,400]{1,0:T(8,128)} %relation.1, s32[2,512]{1,0:T(2,128)} %heads.1, s32[2,512]{1,0:T(2,128)} %tails.1, s32[2,1,256]{2,1,0:T(1,128)} %negs.1, s32[2,512]{1,0:T(2,128)} %relation_ids.1), custom_call_target="tpu_custom_call" | custom-call | tf_op jit(solution)/shard_map/whole_step/pallas_call | solution.py:579
  118.8 1.0 multiply_reduce_fusion
  119.8 0.0 copy-done.2
  119.8 0.5 fusion
  120.3 0.0 copy-done
  120.3 1.5 %divide_subtract_fusion = f32[29,400]{1,0:T(8,128)} fusion(f32[29,400]{1,0:T(8,128)S(1)} %copy-done, f32[32,512]{1,0:T(8,128)} %get-tuple-element.9, f32[29]{0:T(128)S(1)} %get-tuple-element.10), kind=kLoop, calls=%fused_computation | loop fusion | flops 34800 | bytes 139316 | tf_op jit(solution)/shard_map/sub | solution.py:611
  121.9 0.0 copy-start.1
  121.9 4.0 %copy.14 = f32[2048,400]{0,1:T(8,128)} copy(f32[2048,400]{0,1:T(8,128)} %bitcast.4) | data formatting | bytes 6553600
  125.9 0.0 copy-done.1
  125.9 0.6 copy.15
Async XLA Ops:
  0.6 119.7 %copy-start = (f32[29,400]{1,0:T(8,128)S(1)}, f32[29,400]{1,0:T(8,128)}, u32[]{:S(2)}) copy-start(f32[29,400]{1,0:T(8,128)} %relation.1) | copy-start | bytes 139204
  0.6 119.1 %copy-start.2 = (f32[29]{0:T(128)S(1)}, f32[29]{0:T(128)}, u32[]{:S(2)}) copy-start(f32[29]{0:T(128)} %param.11) | copy-start | bytes 352
  121.9 4.0 %copy-start.1 = (f32[1,2048]{1,0:T(1,128)S(1)}, f32[1,2048]{1,0:T(1,128)}, u32[]{:S(2)}) copy-start(f32[1,2048]{1,0:T(1,128)} %get-tuple-element.8) | copy-start | bytes 24580

commit v6 on v5

--- a/solution.py
+++ b/solution.py
@@ -459,15 +459,15 @@
     def _(j):
         m.within[j] = rel_pair(j, at.xl, 8 + j)
 
+        @pl.when(j < 4)
+        def _():
+            head_pair(j)
+
     @pl.loop(0, 8)
     def _(j):
         z_step(j)
 
-        @pl.when(j < 4)
-        def _():
-            head_pair(j)
-
-        @pl.when(j == 4)
+        @pl.when(j == 2)
         def _():
             for b in range(2):
                 for n in range(3):

time: 128 us -> 125 us (0.977); the launches traced: 126 us -> 125 us
    pallas_call x1, Pallas kernels: 118 us -> 117 us  [whole_step(): pl.pallas_call(step_kernel, out_shape=(jax.ShapeDtypeStruct((SLOT, 512),...]
where the time goes in v6:
time: 125 us
  Pallas kernels  117 us (94%)
  local copies, waits for them, and re-layouts  4.63 us (4%)
  other arithmetic  3.02 us (2%)
    pallas_call x1, Pallas kernels, whole_step(): pl.pallas_call(step_kernel, out_shape=(jax.ShapeDtypeStruct((SLOT, 512),...  117 us
    unnamed x8, local copies, waits for them, and re-layouts  4.63 us

profile of v6, /device:TPU:1, one launch (start us, length us, event | category | flops | bytes accessed | tf_op | source)
XLA Modules:
  0.0 124.8 jit_solution(9221183959631627093)
XLA Ops:
  0.6 0.0 copy-start
  0.6 0.0 copy-start.2
  0.7 116.5 %whole_step.1 = (f32[32,512]{1,0:T(8,128)}, f32[400,2048]{1,0:T(8,128)}, f32[1,2048]{1,0:T(1,128)}) custom-call(f32[400,2048]{1,0:T(8,128)} %bitcast.5, f32[1,2048]{1,0:T(1,128)} %bitcast.6, f32[29,400]{1,0:T(8,128)} %relation.1, s32[2,512]{1,0:T(2,128)} %heads.1, s32[2,512]{1,0:T(2,128)} %tails.1, s32[2,1,256]{2,1,0:T(1,128)} %negs.1, s32[2,512]{1,0:T(2,128)} %relation_ids.1), custom_call_target="tpu_custom_call" | custom-call | tf_op jit(solution)/shard_map/whole_step/pallas_call | solution.py:579
  117.2 1.0 multiply_reduce_fusion
  118.1 0.0 copy-done.2
  118.2 0.5 fusion
  118.7 0.0 copy-done
  118.7 1.5 %divide_subtract_fusion = f32[29,400]{1,0:T(8,128)} fusion(f32[29,400]{1,0:T(8,128)S(1)} %copy-done, f32[32,512]{1,0:T(8,128)} %get-tuple-element.9, f32[29]{0:T(128)S(1)} %get-tuple-element.10), kind=kLoop, calls=%fused_computation | loop fusion | flops 34800 | bytes 139316 | tf_op jit(solution)/shard_map/sub | solution.py:611
  120.2 0.0 copy-start.1
  120.2 4.0 %copy.14 = f32[2048,400]{0,1:T(8,128)} copy(f32[2048,400]{0,1:T(8,128)} %bitcast.4) | data formatting | bytes 6553600
  124.2 0.0 copy-done.1
  124.2 0.6 copy.15
Async XLA Ops:
  0.6 118.0 %copy-start = (f32[29,400]{1,0:T(8,128)S(1)}, f32[29,400]{1,0:T(8,128)}, u32[]{:S(2)}) copy-start(f32[29,400]{1,0:T(8,128)} %relation.1) | copy-start | bytes 139204
  0.6 117.5 %copy-start.2 = (f32[29]{0:T(128)S(1)}, f32[29]{0:T(128)}, u32[]{:S(2)}) copy-start(f32[29]{0:T(128)} %param.11) | copy-start | bytes 352
  120.2 4.0 %copy-start.1 = (f32[1,2048]{1,0:T(1,128)S(1)}, f32[1,2048]{1,0:T(1,128)}, u32[]{:S(2)}) copy-start(f32[1,2048]{1,0:T(1,128)} %get-tuple-element.8) | copy-start | bytes 24580
